TPU v7x, 512 devices: a whole 4x4x16 slice. The times are simulated.
512 devices in a mesh: layer: 16 (over z_lo, x), latent: 32 (over z_hi, y, core).
Axes of the slice: x: 4, y: 4, z: 16 (z_hi: 4, z_lo: 4; z = z_hi * 4 + z_lo), core: 2. Of those that a mesh axis runs over, the one named last changes fastest.
Arguments:
- residual: bfloat16 [16, 512, 1024], P('layer', 'latent'), may hold values from -6 to 6
- targets: bfloat16 [16, 512, 1024], P('layer', 'latent'), may hold values from -6 to 6
- enc_weight: bfloat16 [16, 1024, 12288], P('layer', None, 'latent'), may hold values from -0.1875 to 0.1875
- enc_bias: float32 [16, 12288], P('layer', 'latent'), may hold values from -3 to 3
- dec_weight: bfloat16 [16, 2, 12288, 1024], P('layer', None, 'latent'), may hold values from -0.0390625 to 0.0390625
Outputs:
- recon: bfloat16 [16, 512, 1024], P('layer', 'latent')
- dec_grad: bfloat16 [16, 2, 12288, 1024], P('layer', None, 'latent')
- latent_grad: bfloat16 [16, 512, 12288], P('layer', None, 'latent')
All inputs are finite; a program needn't handle non-finite values.
Results may differ from a plain program's by a relative error of at most 0.0053.
Values may be sent and summed in bfloat16 or wider, within the bound.
No kernel may reach another device: no remote copies, remote signals or barrier semaphores. Data moves between devices by JAX's collectives and lax.ppermute only.
A program may use at most 64 MiB of HBM per device.

v0:
```python
import jax
import jax.numpy as jnp
from jax import lax
from jax.sharding import PartitionSpec as P


def shifted(block, axis, distance):
    devices = range(lax.axis_size(axis))
    route = [(i - distance, i) for i in devices if i - distance in devices]
    return lax.ppermute(block, axis, route)


def per_device(residual, targets, enc_weight, enc_bias, dec_weight):
    rows_local = residual[0]
    w_encode = enc_weight[0]
    bias_row = enc_bias[0]
    decoder = dec_weight[0]
    span_count = decoder.shape[0]
    feat_width = decoder.shape[2]
    local_rows = rows_local.shape[0]
    pre = (
        jnp.dot(
            lax.all_gather(rows_local, "latent", axis=0, tiled=True),
            w_encode,
            preferred_element_type=jnp.float32,
        )
        + bias_row
    )
    latents = jax.nn.relu(pre).astype(jnp.bfloat16)
    terms = jnp.einsum("rk,skd->rsd", latents, decoder, preferred_element_type=jnp.float32)
    summed = lax.psum_scatter(
        terms.reshape(local_rows * lax.axis_size("latent"), span_count * feat_width),
        "latent",
        scatter_dimension=0,
        tiled=True,
    )
    total = summed[:, :feat_width]
    offset = 1
    block = summed[:, offset * feat_width : (offset + 1) * feat_width]
    total = total + shifted(block, "layer", offset)
    error = (0.25 * (total - targets[0].astype(jnp.float32))).astype(jnp.bfloat16)
    whole = lax.all_gather(error, "latent", axis=0, tiled=True)
    pieces = [whole]
    offset = 1
    pieces.append(shifted(whole, "layer", -offset))
    stacked = jnp.stack(pieces, axis=1)
    grad_sum = jnp.einsum("rk,rsd->skd", latents, stacked, preferred_element_type=jnp.float32)
    lat_grad = jnp.einsum("rsd,skd->rk", stacked, decoder, preferred_element_type=jnp.float32)
    return (
        total.astype(jnp.bfloat16)[None],
        grad_sum.astype(jnp.bfloat16)[None],
        lat_grad.astype(jnp.bfloat16)[None],
    )


def solution(mesh):
    return jax.shard_map(
        per_device,
        mesh=mesh,
        in_specs=(
            P("layer", "latent", None),
            P("layer", "latent", None),
            P("layer", None, "latent"),
            P("layer", "latent"),
            P("layer", None, "latent", None),
        ),
        out_specs=(
            P("layer", "latent", None),
            P("layer", None, "latent", None),
            P("layer", None, "latent"),
        ),
        check_vma=False,
    )
```

profile of v0, /device:TPU:6, one launch (start us, length us, event | category | flops | bytes accessed | tf_op | source)
XLA Modules:
  0.0 342.9 jit_solution(14329860785346248309)
XLA Ops:
  7.2 0.0 copy-start
  7.2 0.0 copy-start.3
  7.2 0.0 all-gather.6.cloned.1.call-start
  7.2 0.7 all-gather.6.cloned.1.call-update
  7.9 0.0 reduce-scatter.2.cloned.1.call-start
  8.0 1.9 copy.10
  9.9 0.0 copy-done.3
  9.9 77.4 %all-gather.6.cloned.1.call-done = bf16[1,512,1024]{2,1,0:T(8,128)(2,1)} async-done(((bf16[1,16,1024]{2,1,0:T(8,128)(2,1)}), bf16[1,512,1024]{2,1,0:T(8,128)(2,1)}) %all-gather.6.cloned.1.call-update) | async-done | bytes 1048592 | tf_op jit(solution)/shard_map/all_gather | solution.py:23
  87.3 0.0 copy-done
  87.3 1.9 fusion.7
  89.3 3.2 fusion.21
  92.5 0.0 copy-start.2
  92.5 0.0 copy-start.1
  92.5 0.0 reduce-scatter.2.cloned.1.call-update
  92.5 0.0 all-gather.4.cloned.1.call-start
  92.6 133.5 %reduce-scatter.2.cloned.1.call-done = f32[16,2048]{1,0:T(8,128)} async-done(((f32[512,2048]{1,0:T(8,128)}), f32[16,2048]{1,0:T(8,128)}) %reduce-scatter.2.cloned.1.call-update) | async-done | bytes 131088 | tf_op jit(solution)/shard_map/reduce_scatter | solution.py:31
  226.1 0.8 slice.9
  226.9 1.9 collective-permute-start
  228.8 4.2 %collective-permute-done = f32[16,1024]{1,0:T(8,128)S(1)} collective-permute-done((f32[16,1024]{1,0:T(8,128)S(1)}, f32[16,1024]{1,0:T(8,128)S(1)}, u32[]{:S(2)}, u32[]{:S(2)}) %collective-permute-start) | collective-permute-done | bytes 65568 | tf_op jit(solution)/shard_map/ppermute | solution.py:10
  233.1 0.0 copy-done.2
  233.1 1.5 fusion.18
  234.6 0.0 all-gather.4.cloned.1.call-update
  234.6 66.0 %all-gather.4.cloned.1.call-done = bf16[512,1024]{1,0:T(8,128)(2,1)} async-done(((bf16[16,1024]{1,0:T(8,128)(2,1)}), bf16[512,1024]{1,0:T(8,128)(2,1)}) %all-gather.4.cloned.1.call-update) | async-done | bytes 1048592 | tf_op jit(solution)/shard_map/all_gather | solution.py:42
  300.6 2.8 collective-permute-start.1
  303.4 26.8 %collective-permute-done.1 = bf16[512,1024]{1,0:T(8,128)(2,1)S(1)} collective-permute-done((bf16[512,1024]{1,0:T(8,128)(2,1)}, bf16[512,1024]{1,0:T(8,128)(2,1)S(1)}, u32[]{:S(2)}, u32[]{:S(2)}) %collective-permute-start.1) | collective-permute-done | bytes 1048608 | tf_op jit(solution)/shard_map/ppermute | solution.py:10
  330.1 0.0 copy-done.1
  330.1 0.0 copy-start.4
  330.1 3.3 fusion.11
  333.5 0.0 copy-done.4
  333.5 1.3 fusion.2
  334.8 1.6 copy.13
  (1 shorter events, 0.0 us)
Async XLA Ops:
  7.2 80.2 %copy-start = (bf16[1,1024,384]{2,1,0:T(8,128)(2,1)S(1)}, bf16[1,1024,384]{2,1,0:T(8,128)(2,1)}, u32[]{:S(2)}) copy-start(bf16[1,1024,384]{2,1,0:T(8,128)(2,1)} %param.7) | copy-start | bytes 2359300
  7.2 2.7 copy-start.3
  7.2 80.1 %all-gather.6.cloned.1.call-start = ((), (), s32[]{:S(2)}) async-start(), calls=%async_computation.3 | async-start | bytes 1081344 | tf_op jit(solution)/shard_map/all_gather | solution.py:23
  7.9 218.2 %reduce-scatter.2.cloned.1.call-start = ((), (), s32[]{:S(2)}) async-start(), calls=%async_computation.1 | async-start | bytes 4325376 | tf_op jit(solution)/shard_map/reduce_scatter | solution.py:31
  92.5 140.6 %copy-start.2 = (bf16[1,16,1024]{2,1,0:T(8,128)(2,1)S(1)}, bf16[1,16,1024]{2,1,0:T(8,128)(2,1)}, u32[]{:S(2)}) copy-start(bf16[1,16,1024]{2,1,0:T(8,128)(2,1)} %param.6) | copy-start | bytes 98308
  92.5 237.6 %copy-start.1 = (bf16[1,2,384,1024]{3,2,1,0:T(8,128)(2,1)S(1)}, bf16[1,2,384,1024]{3,2,1,0:T(8,128)(2,1)}, u32[]{:S(2)}) copy-start(bf16[1,2,384,1024]{3,2,1,0:T(8,128)(2,1)} %param.9) | copy-start | bytes 4718596
  92.5 208.1 %all-gather.4.cloned.1.call-start = ((), (), s32[]{:S(2)}) async-start(), calls=%async_computation.2 | async-start | bytes 1081344 | tf_op jit(solution)/shard_map/all_gather | solution.py:42
  226.9 6.1 %collective-permute-start = (f32[16,1024]{1,0:T(8,128)S(1)}, f32[16,1024]{1,0:T(8,128)S(1)}, u32[]{:S(2)}, u32[]{:S(2)}) collective-permute-start(f32[16,1024]{1,0:T(8,128)S(1)} %slice.9), channel_id=1, source_target_pairs={{0,32},{32,64},{64,96},{96,128},{128,160},{160,192},{192,224},{224... | collective-permute-start | bytes 196616 | tf_op jit(solution)/shard_map/ppermute | solution.py:10
  300.6 29.5 %collective-permute-start.1 = (bf16[512,1024]{1,0:T(8,128)(2,1)}, bf16[512,1024]{1,0:T(8,128)(2,1)S(1)}, u32[]{:S(2)}, u32[]{:S(2)}) collective-permute-start(bf16[512,1024]{1,0:T(8,128)(2,1)} %all-gather.4.cloned.1.call-done), channel_id=1, source_target_pairs={{32,0},{64,32},{96,64},{128,96},{160,128},{192,160},{224,192},{256... | collective-permute-start | bytes 3145736 | tf_op jit(solution)/shard_map/ppermute | solution.py:10
  330.1 3.3 copy-start.4
Sparse Core Ops, SparseCore 0:
  11.2 76.1 all-gather.5
  92.7 133.3 reduce-scatter.1
  234.7 65.8 all-gather.3
where the time goes:
time: 343 us
  waiting for transfers between devices  309 us (90%)
  between operations  13.8 us (4%)
  matrix products  9.81 us (3%)
  starting transfers between devices  4.79 us (1%)
  local copies, waits for them, and re-layouts  4.37 us (1%)
    reduce_scatter x1, waiting for transfers between devices, per_device(): lax.psum_scatter(terms.reshape(local_rows * lax.axis_size('latent'), span...  133 us
    all_gather x1, waiting for transfers between devices, per_device(): lax.all_gather(rows_local, 'latent', axis=0, tiled=True)  77.4 us
    all_gather x1, waiting for transfers between devices, per_device(): whole = lax.all_gather(error, 'latent', axis=0, tiled=True)  66 us
    ppermute x2, waiting for transfers between devices, shifted(): return lax.ppermute(block, axis, route)  31 us
  transfers between devices with their start and end apart: 5, of which 5 were waited for; matrix products, arithmetic and copies ran while one was open for 1% of the time, Pallas kernels for 0%

commit v1 on v0

v1 whole, which is shorter than its diff:
```python
import jax
import jax.numpy as jnp
from jax import lax
from jax.sharding import Mesh, PartitionSpec as P

BF = jnp.bfloat16
F32 = jnp.float32


def swap_cores(block):
    return lax.ppermute(block, "core", [(0, 1), (1, 0)])


def exchange_z(block, first, second):
    route = [
        (2 * z + c, 2 * (z ^ (second if c else first)) + c)
        for z in range(lax.axis_size("zh"))
        for c in range(2)
    ]
    return lax.ppermute(block, ("zh", "core"), route)


def shift_layer(block, distance):
    count = lax.axis_size(("zl", "x"))
    route = [(i, i + distance) for i in range(count) if 0 <= i + distance < count]
    return lax.ppermute(block, ("zl", "x"), route)


def per_device(residual, targets, enc_weight, enc_bias, dec_weight):
    w_encode = enc_weight[0]
    bias_row = enc_bias[0]
    decoder = dec_weight[0]
    target = targets[0].astype(F32)
    z_at = lax.axis_index("zh") * 16
    core = lax.axis_index("core")

    mine = lax.all_gather(residual[0], "zh", axis=0, tiled=True)
    mine = lax.all_gather(mine, "y", axis=0, tiled=True)
    other = swap_cores(mine)

    def encode(rows):
        pre = jnp.dot(rows, w_encode, preferred_element_type=F32) + bias_row
        return jax.nn.relu(pre).astype(BF)

    lat_mine = encode(mine)
    lat_other = encode(other)

    def decode(lat):
        return jnp.concatenate(
            [jnp.dot(lat, decoder[s], preferred_element_type=F32) for s in range(2)], axis=1
        )

    received = swap_cores(decode(lat_other).astype(BF))
    part = (decode(lat_mine) + received.astype(F32)).astype(BF)
    part = lax.all_to_all(part, "y", 0, 0, tiled=True)
    part = jnp.sum(part.reshape(4, 64, 2048).astype(F32), axis=0)
    shifted = shift_layer(part[:, 1024:].astype(BF), 1)
    part = part[:, :1024] + shifted.astype(F32)
    own = lax.dynamic_slice(part, (z_at, 0), (16, 1024)) - target
    part = lax.dynamic_update_slice(part, own, (z_at, 0))
    part = part + exchange_z(part.astype(BF), 1, 3).astype(F32)
    part = part + exchange_z(part.astype(BF), 3, 1).astype(F32)
    recon = (lax.dynamic_slice(part, (z_at, 0), (16, 1024)) + target).astype(BF)

    error = (0.25 * part).astype(BF)
    both = jnp.stack([error, shift_layer(error, -1)])
    both = jnp.broadcast_to(both, (4, 2, 64, 1024))
    mine_err = lax.all_to_all(both, "y", 0, 0, tiled=True).reshape(512, 1024)
    other_err = swap_cores(mine_err)

    def tokens(a, b):
        a0 = jnp.where(core == 0, a, b)
        a1 = jnp.where(core == 0, b, a)
        st = jnp.stack([a0, a1], axis=1)
        return st

    def split(err):
        err = err.reshape(4, 2, 64, 1024)
        return err[:, 0].reshape(256, 1024), err[:, 1].reshape(256, 1024)

    e_mine, e_other = split(mine_err), split(other_err)
    lat_grad = []
    for e in (e_mine, e_other):
        lat_grad.append(
            sum(
                lax.dot_general(e[s], decoder[s], (((1,), (1,)), ((), ())), preferred_element_type=F32)
                for s in range(2)
            )
            .astype(BF)
            .reshape(4, 4, 16, 384)
        )
    first = jnp.where(core == 0, lat_grad[0], lat_grad[1])
    second = jnp.where(core == 0, lat_grad[1], lat_grad[0])
    lat_out = jnp.stack([first, second], axis=2).transpose(1, 0, 2, 3, 4).reshape(512, 384)
    dec_grad = []
    for s in range(2):
        total = sum(
            lax.dot_general(lat, e[s], (((0,), (0,)), ((), ())), preferred_element_type=F32)
            for lat, e in ((lat_mine, e_mine), (lat_other, e_other))
        )
        dec_grad.append(total.astype(BF))
    return recon[None], jnp.stack(dec_grad)[None], lat_out[None]


def solution(mesh):
    grid = Mesh(mesh.devices.reshape(4, 4, 4, 4, 2), ("zl", "x", "zh", "y", "core"))
    layer, latent = ("zl", "x"), ("zh", "y", "core")
    return jax.shard_map(
        per_device,
        mesh=grid,
        in_specs=(
            P(layer, latent, None),
            P(layer, latent, None),
            P(layer, None, latent),
            P(layer, latent),
            P(layer, None, latent, None),
        ),
        out_specs=(
            P(layer, latent, None),
            P(layer, None, latent, None),
            P(layer, None, latent),
        ),
        check_vma=False,
    )
```

time: 343 us -> 137 us (0.40)
  waiting for transfers between devices: 309 us -> 41.5 us
  blocking collectives: 0 us -> 58.4 us
  starting transfers between devices: 4.79 us -> 22.1 us
  between operations: 13.8 us -> 0.95 us
  matrix products: 9.81 us -> 6.03 us
    all_gather x2 -> x0, waiting for transfers between devices: 143 us -> none  [the longest x1 77.4 us: per_device(): lax.all_gather(rows_local, 'latent', axis=0, tiled=True)]
    reduce_scatter x1 -> x0, waiting for transfers between devices: 133 us -> none  [per_device(): lax.psum_scatter(terms.reshape(local_rows * lax.axis_size('latent'), span...]
    all_gather x0 -> x2, blocking collectives: none -> 39.6 us  [the longest x1 26.2 us: per_device(): mine = lax.all_gather(residual[0], 'zh', axis=0, tiled=True)]
    all_to_all x0 -> x1, blocking collectives: none -> 18.8 us  [per_device(): part = lax.all_to_all(part, 'y', 0, 0, tiled=True)]
    ppermute x2 -> x7, starting transfers between devices: 4.67 us -> 18.6 us  [the longest x2 7.17 us: exchange_z(): return lax.ppermute(block, ('zh', 'core'), route)]
    all_to_all x0 -> x1, waiting for transfers between devices: none -> 9.38 us  [per_device(): mine_err = lax.all_to_all(both, 'y', 0, 0, tiled=True).reshape(512, 1024)]
    dot_general x4 -> x14, matrix products: 9.81 us -> 6.03 us  [the longest x4 1.84 us: per_device(): lax.dot_general(e[s], decoder[s], (((1,), (1,)), ((), ())), preferred_ele...]
    all_to_all x0 -> x1, starting transfers between devices: none -> 3.52 us  [per_device(): mine_err = lax.all_to_all(both, 'y', 0, 0, tiled=True).reshape(512, 1024)]
  transfers between devices with their start and end apart: 5 -> 8, of which waited for: 5 -> 8; matrix products, arithmetic and copies ran while one was open for 1% -> 4% of each run, Pallas kernels for 0% -> 0%
where the time goes in v1:
time: 137 us; the launch traced here: 136 us
  blocking collectives  58.4 us (43%)
  waiting for transfers between devices  41.5 us (30%)
  starting transfers between devices  22.1 us (16%)
  matrix products  6.03 us (4%)
  other arithmetic  4.89 us (4%)
  local copies, waits for them, and re-layouts  2.31 us (2%)
    all_gather x1, blocking collectives, per_device(): mine = lax.all_gather(residual[0], 'zh', axis=0, tiled=True)  26.2 us
    all_to_all x1, blocking collectives, per_device(): part = lax.all_to_all(part, 'y', 0, 0, tiled=True)  18.8 us
    ppermute x2, waiting for transfers between devices, exchange_z(): return lax.ppermute(block, ('zh', 'core'), route)  18.8 us
    all_gather x1, blocking collectives, per_device(): mine = lax.all_gather(mine, 'y', axis=0, tiled=True)  13.4 us
    ppermute x2, waiting for transfers between devices, shift_layer(): return lax.ppermute(block, ('zl', 'x'), route)  10.2 us
    all_to_all x1, waiting for transfers between devices, per_device(): mine_err = lax.all_to_all(both, 'y', 0, 0, tiled=True).reshape(512, 1024)  9.38 us
    ppermute x2, starting transfers between devices, exchange_z(): return lax.ppermute(block, ('zh', 'core'), route)  7.17 us
    ppermute x3, starting transfers between devices, swap_cores(): return lax.ppermute(block, 'core', [(0, 1), (1, 0)])  5.87 us
  transfers between devices with their start and end apart: 8, of which 8 were waited for; matrix products, arithmetic and copies ran while one was open for 4% of the time, Pallas kernels for 0%

profile of v1, /device:TPU:6, one launch (start us, length us, event | category | flops | bytes accessed | tf_op | source)
XLA Modules:
  0.0 136.2 jit_solution(13241649879463160044)
XLA Ops:
  0.6 0.0 copy-start
  0.6 0.0 copy-start.1
  0.7 26.2 %all-gather = bf16[1,64,1024]{2,1,0:T(8,128)(2,1)S(1)} all-gather(bf16[1,16,1024]{2,1,0:T(8,128)(2,1)} %param.5), channel_id=2, replica_groups=mesh['zl'=4,'x'=4,'zh'=4,'y'=4,'core'=2] {'zh'}, dimensions={1}, use_global_device_ids=true | all-gather | bytes 163840 | tf_op jit(solution)/shard_map/all_gather | solution.py:37
  26.8 13.4 %all-gather.1 = bf16[1,256,1024]{2,1,0:T(8,128)(2,1)S(1)} all-gather(bf16[1,64,1024]{2,1,0:T(8,128)(2,1)S(1)} %all-gather), channel_id=3, replica_groups=mesh['zl'=4,'x'=4,'zh'=4,'y'=4,'core'=2] {'y'}, dimensions={1}, use_global_device_ids=true | all-gather | bytes 655360 | tf_op jit(solution)/shard_map/all_gather | solution.py:38
  40.2 1.9 %collective-permute-start = (bf16[256,1024]{1,0:T(8,128)(2,1)S(1)}, bf16[256,1024]{1,0:T(8,128)(2,1)S(1)}, u32[]{:S(2)}, u32[]{:S(2)}) collective-permute-start(bf16[256,1024]{1,0:T(8,128)(2,1)S(1)} %bitcast.82), channel_id=1, source_target_pairs={{0,1},{1,0},{2,3},{3,2},{4,5},{5,4},{6,7},{7,6},{8,9},{9,8},{10,11... | collective-permute-start | bytes 1572872 | tf_op jit(solution)/shard_map/ppermute | solution.py:11
  42.2 0.7 reduce
  42.9 1.2 collective-permute-done
  44.0 0.0 copy-done
  44.0 0.4 fusion.5
  44.5 0.0 copy-done.1
  44.5 0.0 copy-start.2
  44.5 0.4 convolution_convert_fusion
  45.0 0.2 copy-done.2
  45.2 0.4 convolution_convert_fusion.1
  45.6 0.1 pad_maximum_fusion
  45.7 2.0 %collective-permute-start.1 = (bf16[256,2048]{1,0:T(8,128)(2,1)S(1)}, bf16[256,2048]{1,0:T(8,128)(2,1)S(1)}, u32[]{:S(2)}, u32[]{:S(2)}) collective-permute-start(bf16[256,2048]{1,0:T(8,128)(2,1)S(1)} %pad_maximum_fusion), channel_id=1, source_target_pairs={{0,1},{1,0},{2,3},{3,2},{4,5},{5,4},{6,7},{7,6},{8,9},{9,8},{10,11... | collective-permute-start | bytes 3145736 | tf_op jit(solution)/shard_map/ppermute | solution.py:11
  47.8 0.4 fusion.6
  48.2 0.0 copy-start.4
  48.2 0.4 fusion.13
  48.7 0.4 fusion.19
  49.1 0.0 copy-done.4
  49.1 1.1 collective-permute-done.1
  50.3 0.3 fusion
  50.6 18.8 %all_to_all.14 = bf16[4,64,2048]{2,1,0:T(8,128)(2,1)S(1)} all-to-all(bf16[4,64,2048]{2,1,0:T(8,128)(2,1)S(1)} %bitcast.72), channel_id=1, replica_groups=mesh['zl'=4,'x'=4,'zh'=4,'y'=4,'core'=2] {'y'}, dimensions={0} | all-to-all | bytes 2097152 | tf_op jit(solution)/shard_map/all_to_all | solution.py:55
  69.4 0.0 copy-start.6
  69.4 0.2 convert_reduce_fusion
  69.6 2.8 %collective-permute-start.2 = (bf16[64,1024]{1,0:T(8,128)(2,1)S(1)}, bf16[64,1024]{1,0:T(8,128)(2,1)S(1)}, u32[]{:S(2)}, u32[]{:S(2)}) collective-permute-start(bf16[64,1024]{1,0:T(8,128)(2,1)S(1)} %slice.81), channel_id=1, source_target_pairs={{0,32},{32,64},{64,96},{96,128},{128,160},{160,192},{192,224},{224... | collective-permute-start | bytes 393224 | tf_op jit(solution)/shard_map/ppermute | solution.py:26
  72.5 4.0 %collective-permute-done.2 = bf16[64,1024]{1,0:T(8,128)(2,1)S(1)} collective-permute-done((bf16[64,1024]{1,0:T(8,128)(2,1)S(1)}, bf16[64,1024]{1,0:T(8,128)(2,1)S(1)}, u32[]{:S(2)}, u32[]{:S(2)}) %collective-permute-start.2) | collective-permute-done | bytes 131104 | tf_op jit(solution)/shard_map/ppermute | solution.py:26
  76.5 0.0 copy-done.6
  76.6 4.3 %collective-permute-start.3 = (bf16[64,1024]{1,0:T(8,128)(2,1)S(1)}, bf16[64,1024]{1,0:T(8,128)(2,1)S(1)}, u32[]{:S(2)}, u32[]{:S(2)}) collective-permute-start(bf16[64,1024]{1,0:T(8,128)(2,1)S(1)} %convert_element_type.64), channel_id=1, source_target_pairs={{0,8},{1,25},{8,0},{9,17},{16,24},{17,9},{24,16},{25,1},{2,10},{3,... | collective-permute-start | bytes 393224 | tf_op jit(solution)/shard_map/ppermute | solution.py:20
  80.9 10.7 %collective-permute-done.3 = bf16[64,1024]{1,0:T(8,128)(2,1)S(1)} collective-permute-done((bf16[64,1024]{1,0:T(8,128)(2,1)S(1)}, bf16[64,1024]{1,0:T(8,128)(2,1)S(1)}, u32[]{:S(2)}, u32[]{:S(2)}) %collective-permute-start.3) | collective-permute-done | bytes 131104 | tf_op jit(solution)/shard_map/ppermute | solution.py:20
  91.6 2.9 %collective-permute-start.4 = (bf16[64,1024]{1,0:T(8,128)(2,1)S(1)}, bf16[64,1024]{1,0:T(8,128)(2,1)S(1)}, u32[]{:S(2)}, u32[]{:S(2)}) collective-permute-start(bf16[64,1024]{1,0:T(8,128)(2,1)S(1)} %fusion.31), channel_id=1, source_target_pairs={{0,24},{1,9},{8,16},{9,1},{16,8},{17,25},{24,0},{25,17},{2,26},{3,... | collective-permute-start | bytes 393224 | tf_op jit(solution)/shard_map/ppermute | solution.py:20
  94.4 8.1 %collective-permute-done.4 = bf16[64,1024]{1,0:T(8,128)(2,1)S(1)} collective-permute-done((bf16[64,1024]{1,0:T(8,128)(2,1)S(1)}, bf16[64,1024]{1,0:T(8,128)(2,1)S(1)}, u32[]{:S(2)}, u32[]{:S(2)}) %collective-permute-start.4) | collective-permute-done | bytes 131104 | tf_op jit(solution)/shard_map/ppermute | solution.py:20
  102.5 0.8 multiply_convert_fusion
  103.3 2.7 %collective-permute-start.5 = (bf16[64,1024]{1,0:T(8,128)(2,1)S(1)}, bf16[64,1024]{1,0:T(8,128)(2,1)S(1)}, u32[]{:S(2)}, u32[]{:S(2)}) collective-permute-start(bf16[64,1024]{1,0:T(8,128)(2,1)S(1)} %get-tuple-element.3), channel_id=1, source_target_pairs={{32,0},{64,32},{96,64},{128,96},{160,128},{192,160},{224,192},{256... | collective-permute-start | bytes 393224 | tf_op jit(solution)/shard_map/ppermute | solution.py:26
  106.0 6.2 %collective-permute-done.5 = bf16[64,1024]{1,0:T(8,128)(2,1)S(1)} collective-permute-done((bf16[64,1024]{1,0:T(8,128)(2,1)S(1)}, bf16[64,1024]{1,0:T(8,128)(2,1)S(1)}, u32[]{:S(2)}, u32[]{:S(2)}) %collective-permute-start.5) | collective-permute-done | bytes 131104 | tf_op jit(solution)/shard_map/ppermute | solution.py:26
  112.3 1.1 broadcast_in_dim.10
  113.4 3.5 %all-to-all-start.1 = ((bf16[4,2,64,1024]{3,2,1,0:T(8,128)(2,1)}), bf16[4,2,64,1024]{3,2,1,0:T(8,128)(2,1)S(1)}, u32[]{:S(2)}, u32[]{:S(2)}) async-start(bf16[4,2,64,1024]{3,2,1,0:T(8,128)(2,1)} %broadcast_in_dim.10), calls=%async_computation.1 | async-start | bytes 2097152 | tf_op jit(solution)/shard_map/all_to_all | solution.py:68
  116.9 1.5 %fusion.34 = bf16[1,16,1024]{2,1,0:T(8,128)(2,1)} fusion(f32[64,1024]{1,0:T(8,128)} %get-tuple-element.4, s32[]{:T(128)S(6)} %select_n.37, bf16[1,16,1024]{2,1,0:T(8,128)(2,1)S(1)} %copy-done.6), kind=kLoop, calls=%fused_computation.57 | loop fusion | flops 49152 | bytes 131076 | tf_op jit(solution)/shard_map/broadcast_in_dim | solution.py:102
  118.4 9.4 %all-to-all-done.1 = bf16[4,2,64,1024]{3,2,1,0:T(8,128)(2,1)S(1)} async-done(((bf16[4,2,64,1024]{3,2,1,0:T(8,128)(2,1)}), bf16[4,2,64,1024]{3,2,1,0:T(8,128)(2,1)S(1)}, u32[]{:S(2)}, u32[]{:S(2)}) %all-to-all-start.1) | async-done | bytes 1048608 | tf_op jit(solution)/shard_map/all_to_all | solution.py:68
  127.8 1.9 %collective-permute-start.6 = (bf16[512,1024]{1,0:T(8,128)(2,1)S(1)}, bf16[512,1024]{1,0:T(8,128)(2,1)S(1)}, u32[]{:S(2)}, u32[]{:S(2)}) collective-permute-start(bf16[512,1024]{1,0:T(8,128)(2,1)S(1)} %bitcast.71), channel_id=1, source_target_pairs={{0,1},{1,0},{2,3},{3,2},{4,5},{5,4},{6,7},{7,6},{8,9},{9,8},{10,11... | collective-permute-start | bytes 3145736 | tf_op jit(solution)/shard_map/ppermute | solution.py:11
  129.7 0.1 fusion.37
  129.7 0.0 copy-start.5
  129.8 0.5 fusion.16
  130.2 0.5 fusion.7
  130.7 0.0 copy-done.5
  130.7 0.4 fusion.38
  131.1 0.4 fusion.39
  131.5 0.8 collective-permute-done.6
  132.3 0.1 fusion.36
  132.4 0.5 fusion.9
  132.8 0.0 copy-start.3
  132.8 0.5 broadcast_select_fusion.1
  133.4 0.8 copy.8
  134.2 0.0 copy-done.3
  134.2 0.4 fusion.1
  134.6 0.4 fusion.2
  135.0 1.3 maximum_bitcast_fusion
  (7 shorter events, 0.2 us)
Async XLA Ops:
  0.6 43.4 %copy-start = (bf16[1,1024,384]{2,1,0:T(8,128)(2,1)S(1)}, bf16[1,1024,384]{2,1,0:T(8,128)(2,1)}, u32[]{:S(2)}) copy-start(bf16[1,1024,384]{2,1,0:T(8,128)(2,1)} %param.7) | copy-start | bytes 2359300
  0.6 43.8 %copy-start.1 = (bf16[1,2,384,1024]{3,2,1,0:T(8,128)(2,1)S(1)}, bf16[1,2,384,1024]{3,2,1,0:T(8,128)(2,1)}, u32[]{:S(2)}) copy-start(bf16[1,2,384,1024]{3,2,1,0:T(8,128)(2,1)} %param.9) | copy-start | bytes 4718596
  40.2 3.8 %collective-permute-start = (bf16[256,1024]{1,0:T(8,128)(2,1)S(1)}, bf16[256,1024]{1,0:T(8,128)(2,1)S(1)}, u32[]{:S(2)}, u32[]{:S(2)}) collective-permute-start(bf16[256,1024]{1,0:T(8,128)(2,1)S(1)} %bitcast.82), channel_id=1, source_target_pairs={{0,1},{1,0},{2,3},{3,2},{4,5},{5,4},{6,7},{7,6},{8,9},{9,8},{10,11... | collective-permute-start | bytes 1572872 | tf_op jit(solution)/shard_map/ppermute | solution.py:11
  44.5 0.7 copy-start.2
  45.7 4.6 %collective-permute-start.1 = (bf16[256,2048]{1,0:T(8,128)(2,1)S(1)}, bf16[256,2048]{1,0:T(8,128)(2,1)S(1)}, u32[]{:S(2)}, u32[]{:S(2)}) collective-permute-start(bf16[256,2048]{1,0:T(8,128)(2,1)S(1)} %pad_maximum_fusion), channel_id=1, source_target_pairs={{0,1},{1,0},{2,3},{3,2},{4,5},{5,4},{6,7},{7,6},{8,9},{9,8},{10,11... | collective-permute-start | bytes 3145736 | tf_op jit(solution)/shard_map/ppermute | solution.py:11
  48.2 0.9 copy-start.4
  69.4 7.1 %copy-start.6 = (bf16[1,16,1024]{2,1,0:T(8,128)(2,1)S(1)}, bf16[1,16,1024]{2,1,0:T(8,128)(2,1)}, u32[]{:S(2)}) copy-start(bf16[1,16,1024]{2,1,0:T(8,128)(2,1)} %param.6) | copy-start | bytes 98308
  69.6 6.9 %collective-permute-start.2 = (bf16[64,1024]{1,0:T(8,128)(2,1)S(1)}, bf16[64,1024]{1,0:T(8,128)(2,1)S(1)}, u32[]{:S(2)}, u32[]{:S(2)}) collective-permute-start(bf16[64,1024]{1,0:T(8,128)(2,1)S(1)} %slice.81), channel_id=1, source_target_pairs={{0,32},{32,64},{64,96},{96,128},{128,160},{160,192},{192,224},{224... | collective-permute-start | bytes 393224 | tf_op jit(solution)/shard_map/ppermute | solution.py:26
  76.6 15.0 %collective-permute-start.3 = (bf16[64,1024]{1,0:T(8,128)(2,1)S(1)}, bf16[64,1024]{1,0:T(8,128)(2,1)S(1)}, u32[]{:S(2)}, u32[]{:S(2)}) collective-permute-start(bf16[64,1024]{1,0:T(8,128)(2,1)S(1)} %convert_element_type.64), channel_id=1, source_target_pairs={{0,8},{1,25},{8,0},{9,17},{16,24},{17,9},{24,16},{25,1},{2,10},{3,... | collective-permute-start | bytes 393224 | tf_op jit(solution)/shard_map/ppermute | solution.py:20
  91.6 11.0 %collective-permute-start.4 = (bf16[64,1024]{1,0:T(8,128)(2,1)S(1)}, bf16[64,1024]{1,0:T(8,128)(2,1)S(1)}, u32[]{:S(2)}, u32[]{:S(2)}) collective-permute-start(bf16[64,1024]{1,0:T(8,128)(2,1)S(1)} %fusion.31), channel_id=1, source_target_pairs={{0,24},{1,9},{8,16},{9,1},{16,8},{17,25},{24,0},{25,17},{2,26},{3,... | collective-permute-start | bytes 393224 | tf_op jit(solution)/shard_map/ppermute | solution.py:20
  103.3 9.0 %collective-permute-start.5 = (bf16[64,1024]{1,0:T(8,128)(2,1)S(1)}, bf16[64,1024]{1,0:T(8,128)(2,1)S(1)}, u32[]{:S(2)}, u32[]{:S(2)}) collective-permute-start(bf16[64,1024]{1,0:T(8,128)(2,1)S(1)} %get-tuple-element.3), channel_id=1, source_target_pairs={{32,0},{64,32},{96,64},{128,96},{160,128},{192,160},{224,192},{256... | collective-permute-start | bytes 393224 | tf_op jit(solution)/shard_map/ppermute | solution.py:26
  113.4 14.4 %all-to-all-start.1 = ((bf16[4,2,64,1024]{3,2,1,0:T(8,128)(2,1)}), bf16[4,2,64,1024]{3,2,1,0:T(8,128)(2,1)S(1)}, u32[]{:S(2)}, u32[]{:S(2)}) async-start(bf16[4,2,64,1024]{3,2,1,0:T(8,128)(2,1)} %broadcast_in_dim.10), calls=%async_computation.1 | async-start | bytes 2097152 | tf_op jit(solution)/shard_map/all_to_all | solution.py:68
  127.8 4.5 %collective-permute-start.6 = (bf16[512,1024]{1,0:T(8,128)(2,1)S(1)}, bf16[512,1024]{1,0:T(8,128)(2,1)S(1)}, u32[]{:S(2)}, u32[]{:S(2)}) collective-permute-start(bf16[512,1024]{1,0:T(8,128)(2,1)S(1)} %bitcast.71), channel_id=1, source_target_pairs={{0,1},{1,0},{2,3},{3,2},{4,5},{5,4},{6,7},{7,6},{8,9},{9,8},{10,11... | collective-permute-start | bytes 3145736 | tf_op jit(solution)/shard_map/ppermute | solution.py:11
  129.7 0.9 copy-start.5
  132.8 1.3 copy-start.3

commit v2 on v1

v2 whole, which is shorter than its diff:
```python
import jax
import jax.numpy as jnp
from jax import lax
from jax.experimental import pallas as pl
from jax.experimental.pallas import tpu as pltpu
from jax.sharding import PartitionSpec as P

BF = jnp.bfloat16
F32 = jnp.float32


def place(z, y, rows):
    return 8 * z + 2 * y + ((rows ^ z ^ y) & 1)


ALONG_Z = [[place(z, y, r) for z in range(4)] for y in range(4) for r in range(2)]
ALONG_Y = [[place(z, y, r) for y in range(4)] for z in range(4) for r in range(2)]


def swap_cores(block):
    return lax.ppermute(block, "latent", [(i, i ^ 1) for i in range(32)])


def exchange_z(block, first, second):
    route = [
        (place(z, y, r), place(z ^ (second if r else first), y, r))
        for z in range(4)
        for y in range(4)
        for r in range(2)
    ]
    return lax.ppermute(block, "latent", route)


def shift_layer(block, distance):
    count = lax.axis_size("layer")
    route = [(i, i + distance) for i in range(count) if 0 <= i + distance < count]
    return lax.ppermute(block, "layer", route)


VMEM = pl.BlockSpec(memory_space=pltpu.VMEM)
ANYWHERE = pl.BlockSpec(memory_space=pl.ANY)
ACROSS = (((1,), (1,)), ((), ()))


def call(kernel, outs, specs, out_specs, flops, scratch=()):
    return pl.pallas_call(
        kernel,
        out_shape=outs,
        in_specs=specs,
        out_specs=out_specs,
        scratch_shapes=scratch,
        compiler_params=pltpu.CompilerParams(vmem_limit_bytes=32 * 1024 * 1024),
        cost_estimate=pl.CostEstimate(flops=flops, bytes_accessed=2_000_000, transcendentals=0),
    )


def copies_kernel(own_ref, next_ref, out_ref):
    for y in range(4):
        out_ref[y, 0] = own_ref[...]
        out_ref[y, 1] = next_ref[...]


def copies(own, after):
    out = jax.ShapeDtypeStruct((4, 2, 64, 1024), BF)
    return call(copies_kernel, out, [VMEM] * 2, VMEM, 1)(own, after)


def rows_of(err_ref, s):
    return err_ref[:, s].reshape(256, 1024)


def latent_rows(err_ref, dec_ref):
    total = lax.dot_general(rows_of(err_ref, 0), dec_ref[0], ACROSS, preferred_element_type=F32)
    total += lax.dot_general(rows_of(err_ref, 1), dec_ref[1], ACROSS, preferred_element_type=F32)
    return total.astype(BF)


def first_kernel(err_ref, lat_ref, dec_ref, parts_ref, held_ref):
    for s in range(2):
        parts_ref[s] = jnp.dot(lat_ref[...], rows_of(err_ref, s), preferred_element_type=F32)
    held_ref[...] = latent_rows(err_ref, dec_ref)


def first_gradients(err, lat_t, decoder):
    outs = (jax.ShapeDtypeStruct((2, 384, 1024), F32), jax.ShapeDtypeStruct((256, 384), BF))
    return call(first_kernel, outs, [VMEM] * 3, (VMEM, VMEM), 805_306_368)(err, lat_t, decoder)


def last_kernel(set_ref, err_ref, lat_ref, dec_ref, parts_ref, held_ref, dec_out, lat_out, dec_buf, lat_buf, sems):
    even = set_ref[0] * 16
    sends = [pltpu.make_async_copy(dec_buf.at[s], dec_out.at[s], sems.at[s]) for s in range(2)]
    sends.append(pltpu.make_async_copy(lat_buf, lat_out, sems.at[2]))
    for s in range(2):
        total = parts_ref[s] + jnp.dot(lat_ref[...], rows_of(err_ref, s), preferred_element_type=F32)
        dec_buf[s] = total.astype(BF)
        sends[s].start()
    total = latent_rows(err_ref, dec_ref)
    for y in range(4):
        for z in range(4):
            here = y * 64 + z * 16
            there = z * 128 + y * 32
            at = even if (y ^ z) & 1 == 0 else 16 - even
            away = 16 - at
            lat_buf[pl.ds(pl.multiple_of(there + at, 16), 16), :] = held_ref[here : here + 16, :]
            lat_buf[pl.ds(pl.multiple_of(there + away, 16), 16), :] = total[here : here + 16, :]
    sends[2].start()
    for send in sends:
        send.wait()


def last_gradients(row_set, err, lat_t, decoder, parts, held):
    outs = (jax.ShapeDtypeStruct((2, 384, 1024), BF), jax.ShapeDtypeStruct((512, 384), BF))
    specs = [pl.BlockSpec(memory_space=pltpu.SMEM)] + [VMEM] * 5
    scratch = [pltpu.VMEM((2, 384, 1024), BF), pltpu.VMEM((512, 384), BF), pltpu.SemaphoreType.DMA((3,))]
    return call(last_kernel, outs, specs, (ANYWHERE, ANYWHERE), 805_306_368, scratch)(
        row_set.reshape(1), err, lat_t, decoder, parts, held
    )


def per_device(residual, targets, enc_weight, enc_bias, dec_weight):
    w_encode = enc_weight[0]
    bias_row = enc_bias[0]
    decoder = dec_weight[0]
    target = targets[0].astype(F32)
    latent = lax.axis_index("latent")
    z_at = (latent // 8) * 16
    row_set = (latent ^ (latent // 2) ^ (latent // 8)) & 1

    mine = lax.all_gather(residual[0], "latent", axis=0, tiled=True, axis_index_groups=ALONG_Z)
    mine = lax.all_gather(mine, "latent", axis=0, tiled=True, axis_index_groups=ALONG_Y)
    other = swap_cores(mine)

    def encode(rows):
        pre = jnp.dot(rows, w_encode, preferred_element_type=F32) + bias_row
        return jax.nn.relu(pre).astype(BF)

    lat_mine = encode(mine)
    lat_other = encode(other)

    def decode(lat):
        return jnp.concatenate(
            [jnp.dot(lat, decoder[s], preferred_element_type=F32) for s in range(2)], axis=1
        )

    received = swap_cores(decode(lat_other).astype(BF))
    part = (decode(lat_mine) + received.astype(F32)).astype(BF)
    part = lax.all_to_all(part, "latent", 0, 0, tiled=True, axis_index_groups=ALONG_Y)
    part = jnp.sum(part.reshape(4, 64, 2048).astype(F32), axis=0)
    shifted = shift_layer(part[:, 1024:].astype(BF), 1)
    part = part[:, :1024] + shifted.astype(F32)
    own = lax.dynamic_slice(part, (z_at, 0), (16, 1024)) - target
    part = lax.dynamic_update_slice(part, own, (z_at, 0))
    part = part + exchange_z(part.astype(BF), 1, 3).astype(F32)
    part = part + exchange_z(part.astype(BF), 3, 1).astype(F32)
    recon = (lax.dynamic_slice(part, (z_at, 0), (16, 1024)) + target).astype(BF)

    error = (0.25 * part).astype(BF)
    after, recon = lax.optimization_barrier((shift_layer(error, -1), recon))
    both = copies(error, after)
    mine_err = lax.all_to_all(both, "latent", 0, 0, tiled=True, axis_index_groups=ALONG_Y)
    other_err = swap_cores(mine_err)
    parts, held = first_gradients(mine_err, lat_mine.T, decoder)
    dec_grad, lat_grad = last_gradients(row_set, other_err, lat_other.T, decoder, parts, held)
    return recon[None], dec_grad[None], lat_grad[None]


def solution(mesh):
    return jax.shard_map(
        per_device,
        mesh=mesh,
        in_specs=(
            P("layer", "latent", None),
            P("layer", "latent", None),
            P("layer", None, "latent"),
            P("layer", "latent"),
            P("layer", None, "latent", None),
        ),
        out_specs=(
            P("layer", "latent", None),
            P("layer", None, "latent", None),
            P("layer", None, "latent"),
        ),
        check_vma=False,
    )
```

time: 137 us -> 135 us (0.985); the launches traced: 136 us -> 133 us
  blocking collectives: 58.4 us -> 72.5 us
  waiting for transfers between devices: 41.5 us -> 32.2 us
  starting transfers between devices: 22.1 us -> 16.6 us
  Pallas kernels: 0 us -> 4.34 us
  matrix products: 6.03 us -> 2.75 us
  other arithmetic: 4.89 us -> 1.99 us
    all_to_all x1 -> x2, blocking collectives: 18.8 us -> 34.8 us  [the longest x1 19.2 us: per_device(): lax.all_to_all(part, 'latent', 0, 0, tiled=True, axis_index_groups=ALONG_Y)]
    all_to_all x1 -> x0, waiting for transfers between devices: 9.38 us -> none  [per_device(): mine_err = lax.all_to_all(both, 'y', 0, 0, tiled=True).reshape(512, 1024)]
    pallas_call x0 -> x3, Pallas kernels: none -> 4.34 us  [the longest x1 2.38 us: first_gradients(): call(first_kernel, outs, [VMEM] * 3, (VMEM, VMEM), 805306368)]
    all_to_all x1 -> x0, starting transfers between devices: 3.52 us -> none  [per_device(): mine_err = lax.all_to_all(both, 'y', 0, 0, tiled=True).reshape(512, 1024)]
    dot_general x8 -> x0, matrix products: 3.4 us -> none  [the longest x4 1.84 us: per_device(): lax.dot_general(e[s], decoder[s], (((1,), (1,)), ((), ())), preferred_ele...]
    broadcast_in_dim x2 -> x0, other arithmetic: 2.75 us -> none  [per_device(): return (recon[None], jnp.stack(dec_grad)[None], lat_out[None])]
    ppermute x7, starting transfers between devices: 18.6 us -> 16.6 us  [the longest x3 6.41 us: swap_cores(): return lax.ppermute(block, 'latent', [(i, i ^ 1) for i in range(32)])]
    all_gather x2, blocking collectives: 39.6 us -> 37.7 us  [the longest x1 24.9 us: per_device(): lax.all_gather(residual[0], 'latent', axis=0, tiled=True, axis_index_grou...]
  transfers between devices with their start and end apart: 8 -> 7, of which waited for: 8 -> 6; matrix products, arithmetic and copies ran while one was open for 4% -> 2% of each run, Pallas kernels for 0% -> 2%
where the time goes in v2:
time: 135 us; the launch traced here: 133 us
  blocking collectives  72.5 us (54%)
  waiting for transfers between devices  32.2 us (24%)
  starting transfers between devices  16.6 us (12%)
  Pallas kernels  4.34 us (3%)
  matrix products  2.75 us (2%)
  other arithmetic  1.99 us (1%)
  local copies, waits for them, and re-layouts  1.38 us (1%)
    all_gather x1, blocking collectives, per_device(): lax.all_gather(residual[0], 'latent', axis=0, tiled=True, axis_index_grou...  24.9 us
    ppermute x2, waiting for transfers between devices, exchange_z(): return lax.ppermute(block, 'latent', route)  21 us
    all_to_all x1, blocking collectives, per_device(): lax.all_to_all(part, 'latent', 0, 0, tiled=True, axis_index_groups=ALONG_Y)  19.2 us
    all_to_all x1, blocking collectives, per_device(): lax.all_to_all(both, 'latent', 0, 0, tiled=True, axis_index_groups=ALONG_Y)  15.5 us
    all_gather x1, blocking collectives, per_device(): lax.all_gather(mine, 'latent', axis=0, tiled=True, axis_index_groups=ALON...  12.8 us
    ppermute x2, waiting for transfers between devices, shift_layer(): return lax.ppermute(block, 'layer', route)  9.74 us
    ppermute x3, starting transfers between devices, swap_cores(): return lax.ppermute(block, 'latent', [(i, i ^ 1) for i in range(32)])  6.41 us
    ppermute x2, starting transfers between devices, shift_layer(): return lax.ppermute(block, 'layer', route)  5.56 us
  transfers between devices with their start and end apart: 7, of which 6 were waited for; matrix products, arithmetic and copies ran while one was open for 2% of the time, Pallas kernels for 2%

profile of v2, /device:TPU:6, one launch (start us, length us, event | category | flops | bytes accessed | tf_op | source)
XLA Modules:
  0.0 132.7 jit_solution(4638542521614091446)
XLA Ops:
  0.6 0.0 copy-start
  0.6 0.0 copy-start.1
  0.7 24.9 %all-gather = bf16[1,64,1024]{2,1,0:T(8,128)(2,1)S(1)} all-gather(bf16[1,16,1024]{2,1,0:T(8,128)(2,1)} %param.5), channel_id=2, replica_groups={{0,9,16,25},{1,8,17,24},{3,10,19,26},{2,11,18,27},{4,13,20,29},{5,12,21..., dimensions={1}, use_global_device_ids=true | all-gather | bytes 163840 | tf_op jit(solution)/shard_map/all_gather | solution.py:129
  25.5 12.8 %all-gather.1 = bf16[1,256,1024]{2,1,0:T(8,128)(2,1)S(1)} all-gather(bf16[1,64,1024]{2,1,0:T(8,128)(2,1)S(1)} %all-gather), channel_id=3, replica_groups={{0,3,4,7},{1,2,5,6},{9,10,13,14},{8,11,12,15},{16,19,20,23},{17,18,21,2..., dimensions={1}, use_global_device_ids=true | all-gather | bytes 655360 | tf_op jit(solution)/shard_map/all_gather | solution.py:130
  38.4 2.2 %collective-permute-start = (bf16[256,1024]{1,0:T(8,128)(2,1)S(1)}, bf16[256,1024]{1,0:T(8,128)(2,1)S(1)}, u32[]{:S(2)}, u32[]{:S(2)}) collective-permute-start(bf16[256,1024]{1,0:T(8,128)(2,1)S(1)} %bitcast.40), channel_id=1, source_target_pairs={{0,1},{1,0},{2,3},{3,2},{4,5},{5,4},{6,7},{7,6},{8,9},{9,8},{10,11... | collective-permute-start | bytes 1572872 | tf_op jit(solution)/shard_map/ppermute | solution.py:21
  40.6 0.7 reduce
  41.3 0.8 collective-permute-done
  42.1 0.0 copy-done
  42.2 0.5 fusion.3
  42.6 0.0 copy-done.1
  42.6 0.0 copy-start.4
  42.7 0.5 convolution_convert_fusion
  43.1 0.2 copy-done.4
  43.3 0.5 convolution_convert_fusion.1
  43.8 0.1 pad_maximum_fusion
  43.9 2.3 %collective-permute-start.1 = (bf16[256,2048]{1,0:T(8,128)(2,1)S(1)}, bf16[256,2048]{1,0:T(8,128)(2,1)S(1)}, u32[]{:S(2)}, u32[]{:S(2)}) collective-permute-start(bf16[256,2048]{1,0:T(8,128)(2,1)S(1)} %pad_maximum_fusion), channel_id=1, source_target_pairs={{0,1},{1,0},{2,3},{3,2},{4,5},{5,4},{6,7},{7,6},{8,9},{9,8},{10,11... | collective-permute-start | bytes 3145736 | tf_op jit(solution)/shard_map/ppermute | solution.py:21
  46.1 0.5 fusion.4
  46.6 0.0 copy-start.2
  46.6 0.5 fusion.6
  47.1 0.2 copy-done.2
  47.3 0.5 fusion.9
  47.7 0.7 collective-permute-done.1
  48.4 0.3 fusion
  48.7 0.0 copy-start.6
  48.7 19.2 %all_to_all.14 = bf16[4,64,2048]{2,1,0:T(8,128)(2,1)S(1)} all-to-all(bf16[4,64,2048]{2,1,0:T(8,128)(2,1)S(1)} %bitcast.39), channel_id=1, replica_groups={{0,3,4,7},{1,2,5,6},{9,10,13,14},{8,11,12,15},{16,19,20,23},{17,18,21,2..., dimensions={0} | all-to-all | bytes 2097152 | tf_op jit(solution)/shard_map/all_to_all | solution.py:147
  67.9 0.2 convert_reduce_fusion
  68.1 2.8 %collective-permute-start.2 = (bf16[64,1024]{1,0:T(8,128)(2,1)S(1)}, bf16[64,1024]{1,0:T(8,128)(2,1)S(1)}, u32[]{:S(2)}, u32[]{:S(2)}) collective-permute-start(bf16[64,1024]{1,0:T(8,128)(2,1)S(1)} %slice.41), channel_id=1, source_target_pairs={{0,32},{32,64},{64,96},{96,128},{128,160},{160,192},{192,224},{224... | collective-permute-start | bytes 393224 | tf_op jit(solution)/shard_map/ppermute | solution.py:37
  71.0 4.1 %collective-permute-done.2 = bf16[64,1024]{1,0:T(8,128)(2,1)S(1)} collective-permute-done((bf16[64,1024]{1,0:T(8,128)(2,1)S(1)}, bf16[64,1024]{1,0:T(8,128)(2,1)S(1)}, u32[]{:S(2)}, u32[]{:S(2)}) %collective-permute-start.2) | collective-permute-done | bytes 131104 | tf_op jit(solution)/shard_map/ppermute | solution.py:37
  75.2 0.0 copy-done.6
  75.2 2.7 %collective-permute-start.3 = (bf16[64,1024]{1,0:T(8,128)(2,1)S(1)}, bf16[64,1024]{1,0:T(8,128)(2,1)S(1)}, u32[]{:S(2)}, u32[]{:S(2)}) collective-permute-start(bf16[64,1024]{1,0:T(8,128)(2,1)S(1)} %convert_element_type.60), channel_id=1, source_target_pairs={{0,9},{1,24},{3,10},{2,27},{4,13},{5,28},{7,14},{6,31},{9,0},{8,17... | collective-permute-start | bytes 393224 | tf_op jit(solution)/shard_map/ppermute | solution.py:31
  77.9 11.4 %collective-permute-done.3 = bf16[64,1024]{1,0:T(8,128)(2,1)S(1)} collective-permute-done((bf16[64,1024]{1,0:T(8,128)(2,1)S(1)}, bf16[64,1024]{1,0:T(8,128)(2,1)S(1)}, u32[]{:S(2)}, u32[]{:S(2)}) %collective-permute-start.3) | collective-permute-done | bytes 131104 | tf_op jit(solution)/shard_map/ppermute | solution.py:31
  89.4 1.9 %collective-permute-start.4 = (bf16[64,1024]{1,0:T(8,128)(2,1)S(1)}, bf16[64,1024]{1,0:T(8,128)(2,1)S(1)}, u32[]{:S(2)}, u32[]{:S(2)}) collective-permute-start(bf16[64,1024]{1,0:T(8,128)(2,1)S(1)} %fusion.17), channel_id=1, source_target_pairs={{0,25},{1,8},{3,26},{2,11},{4,29},{5,12},{7,30},{6,15},{9,16},{8,1... | collective-permute-start | bytes 393224 | tf_op jit(solution)/shard_map/ppermute | solution.py:31
  91.3 9.5 %collective-permute-done.4 = bf16[64,1024]{1,0:T(8,128)(2,1)S(1)} collective-permute-done((bf16[64,1024]{1,0:T(8,128)(2,1)S(1)}, bf16[64,1024]{1,0:T(8,128)(2,1)S(1)}, u32[]{:S(2)}, u32[]{:S(2)}) %collective-permute-start.4) | collective-permute-done | bytes 131104 | tf_op jit(solution)/shard_map/ppermute | solution.py:31
  100.9 0.1 multiply_convert_fusion
  100.9 2.7 %collective-permute-start.5 = (bf16[64,1024]{1,0:T(8,128)(2,1)S(1)}, bf16[64,1024]{1,0:T(8,128)(2,1)S(1)}, u32[]{:S(2)}, u32[]{:S(2)}) collective-permute-start(bf16[64,1024]{1,0:T(8,128)(2,1)S(1)} %get-tuple-element.15.own_ref), channel_id=1, source_target_pairs={{32,0},{64,32},{96,64},{128,96},{160,128},{192,160},{224,192},{256... | collective-permute-start | bytes 393224 | tf_op jit(solution)/shard_map/ppermute | solution.py:37
  103.7 0.6 fusion.19
  104.3 5.6 %collective-permute-done.5.next_ref = bf16[64,1024]{1,0:T(8,128)(2,1)S(1)} collective-permute-done((bf16[64,1024]{1,0:T(8,128)(2,1)S(1)}, bf16[64,1024]{1,0:T(8,128)(2,1)S(1)}, u32[]{:S(2)}, u32[]{:S(2)}) %collective-permute-start.5) | collective-permute-done | bytes 131104 | tf_op jit(solution)/shard_map/ppermute | solution.py:37
  109.9 0.1 shard_map.76
  110.0 15.5 %all_to_all.15.err_ref = bf16[4,2,64,1024]{3,2,1,0:T(8,128)(2,1)} all-to-all(bf16[4,2,64,1024]{3,2,1,0:T(8,128)(2,1)S(1)} %shard_map.76), channel_id=1, replica_groups={{0,3,4,7},{1,2,5,6},{9,10,13,14},{8,11,12,15},{16,19,20,23},{17,18,21,2..., dimensions={0} | all-to-all | bytes 2097152 | tf_op jit(solution)/shard_map/all_to_all | solution.py:160
  125.5 1.9 %collective-permute-start.6 = (bf16[4,2,64,1024]{3,2,1,0:T(8,128)(2,1)}, bf16[4,2,64,1024]{3,2,1,0:T(8,128)(2,1)S(1)}, u32[]{:S(2)}, u32[]{:S(2)}) collective-permute-start(bf16[4,2,64,1024]{3,2,1,0:T(8,128)(2,1)} %all_to_all.15.err_ref), channel_id=1, source_target_pairs={{0,1},{1,0},{2,3},{3,2},{4,5},{5,4},{6,7},{7,6},{8,9},{9,8},{10,11... | collective-permute-start | bytes 3145736 | tf_op jit(solution)/shard_map/ppermute | solution.py:21
  127.5 0.0 copy-start.3
  127.5 0.9 copy-done.3
  128.4 0.0 copy-start.5
  128.4 2.4 %shard_map.77 = (f32[2,384,1024]{2,1,0:T(8,128)S(1)}, bf16[256,384]{1,0:T(8,128)(2,1)S(1)}) custom-call(bf16[4,2,64,1024]{3,2,1,0:T(8,128)(2,1)} %all_to_all.15.err_ref, bf16[384,256]{1,0:T(8,128)(2,1)S(1)} %bitcast.37, bf16[2,384,1024]{2,1,0:T(8,128)(2,1)S(1)} %bitcast.35), custom_call_target="tpu_custom_call" | custom-call | flops 805306368 | bytes 2000000 | tf_op jit(solution)/shard_map/pallas_call | solution.py:86
  130.8 0.0 collective-permute-done.6.err_ref
  130.8 0.0 copy-done.5
  130.8 1.9 %shard_map.78 = (bf16[2,384,1024]{2,1,0:T(8,128)(2,1)}, bf16[512,384]{1,0:T(8,128)(2,1)}) custom-call(s32[1]{0:T(128)} %bitcast.8.set_ref, bf16[4,2,64,1024]{3,2,1,0:T(8,128)(2,1)S(1)} %collective-permute-done.6.err_ref, bf16[384,256]{1,0:T(8,128)(2,1)S(1)} %bitcast.38, bf16[2,384,1024]{2,1,0:T(8,128)(2,1)S(1)} %bitcast.36, ...), custom_call_target="tpu_custom_call" | custom-call | flops 805306368 | bytes 2000000 | tf_op jit(solution)/shard_map/pallas_call | solution.py:115
  (5 shorter events, 0.1 us)
Async XLA Ops:
  0.6 41.5 %copy-start = (bf16[1,1024,384]{2,1,0:T(8,128)(2,1)S(1)}, bf16[1,1024,384]{2,1,0:T(8,128)(2,1)}, u32[]{:S(2)}) copy-start(bf16[1,1024,384]{2,1,0:T(8,128)(2,1)} %param.7) | copy-start | bytes 2359300
  0.6 42.0 %copy-start.1 = (bf16[1,2,384,1024]{3,2,1,0:T(8,128)(2,1)S(1)}, bf16[1,2,384,1024]{3,2,1,0:T(8,128)(2,1)}, u32[]{:S(2)}) copy-start(bf16[1,2,384,1024]{3,2,1,0:T(8,128)(2,1)} %param.9) | copy-start | bytes 4718596
  38.4 3.8 %collective-permute-start = (bf16[256,1024]{1,0:T(8,128)(2,1)S(1)}, bf16[256,1024]{1,0:T(8,128)(2,1)S(1)}, u32[]{:S(2)}, u32[]{:S(2)}) collective-permute-start(bf16[256,1024]{1,0:T(8,128)(2,1)S(1)} %bitcast.40), channel_id=1, source_target_pairs={{0,1},{1,0},{2,3},{3,2},{4,5},{5,4},{6,7},{7,6},{8,9},{9,8},{10,11... | collective-permute-start | bytes 1572872 | tf_op jit(solution)/shard_map/ppermute | solution.py:21
  42.6 0.7 copy-start.4
  43.9 4.6 %collective-permute-start.1 = (bf16[256,2048]{1,0:T(8,128)(2,1)S(1)}, bf16[256,2048]{1,0:T(8,128)(2,1)S(1)}, u32[]{:S(2)}, u32[]{:S(2)}) collective-permute-start(bf16[256,2048]{1,0:T(8,128)(2,1)S(1)} %pad_maximum_fusion), channel_id=1, source_target_pairs={{0,1},{1,0},{2,3},{3,2},{4,5},{5,4},{6,7},{7,6},{8,9},{9,8},{10,11... | collective-permute-start | bytes 3145736 | tf_op jit(solution)/shard_map/ppermute | solution.py:21
  46.6 0.7 copy-start.2
  48.7 26.4 %copy-start.6 = (bf16[1,16,1024]{2,1,0:T(8,128)(2,1)S(1)}, bf16[1,16,1024]{2,1,0:T(8,128)(2,1)}, u32[]{:S(2)}) copy-start(bf16[1,16,1024]{2,1,0:T(8,128)(2,1)} %param.6) | copy-start | bytes 98308
  68.1 7.0 %collective-permute-start.2 = (bf16[64,1024]{1,0:T(8,128)(2,1)S(1)}, bf16[64,1024]{1,0:T(8,128)(2,1)S(1)}, u32[]{:S(2)}, u32[]{:S(2)}) collective-permute-start(bf16[64,1024]{1,0:T(8,128)(2,1)S(1)} %slice.41), channel_id=1, source_target_pairs={{0,32},{32,64},{64,96},{96,128},{128,160},{160,192},{192,224},{224... | collective-permute-start | bytes 393224 | tf_op jit(solution)/shard_map/ppermute | solution.py:37
  75.2 14.1 %collective-permute-start.3 = (bf16[64,1024]{1,0:T(8,128)(2,1)S(1)}, bf16[64,1024]{1,0:T(8,128)(2,1)S(1)}, u32[]{:S(2)}, u32[]{:S(2)}) collective-permute-start(bf16[64,1024]{1,0:T(8,128)(2,1)S(1)} %convert_element_type.60), channel_id=1, source_target_pairs={{0,9},{1,24},{3,10},{2,27},{4,13},{5,28},{7,14},{6,31},{9,0},{8,17... | collective-permute-start | bytes 393224 | tf_op jit(solution)/shard_map/ppermute | solution.py:31
  89.4 11.5 %collective-permute-start.4 = (bf16[64,1024]{1,0:T(8,128)(2,1)S(1)}, bf16[64,1024]{1,0:T(8,128)(2,1)S(1)}, u32[]{:S(2)}, u32[]{:S(2)}) collective-permute-start(bf16[64,1024]{1,0:T(8,128)(2,1)S(1)} %fusion.17), channel_id=1, source_target_pairs={{0,25},{1,8},{3,26},{2,11},{4,29},{5,12},{7,30},{6,15},{9,16},{8,1... | collective-permute-start | bytes 393224 | tf_op jit(solution)/shard_map/ppermute | solution.py:31
  100.9 9.0 %collective-permute-start.5 = (bf16[64,1024]{1,0:T(8,128)(2,1)S(1)}, bf16[64,1024]{1,0:T(8,128)(2,1)S(1)}, u32[]{:S(2)}, u32[]{:S(2)}) collective-permute-start(bf16[64,1024]{1,0:T(8,128)(2,1)S(1)} %get-tuple-element.15.own_ref), channel_id=1, source_target_pairs={{32,0},{64,32},{96,64},{128,96},{160,128},{192,160},{224,192},{256... | collective-permute-start | bytes 393224 | tf_op jit(solution)/shard_map/ppermute | solution.py:37
  125.5 5.3 %collective-permute-start.6 = (bf16[4,2,64,1024]{3,2,1,0:T(8,128)(2,1)}, bf16[4,2,64,1024]{3,2,1,0:T(8,128)(2,1)S(1)}, u32[]{:S(2)}, u32[]{:S(2)}) collective-permute-start(bf16[4,2,64,1024]{3,2,1,0:T(8,128)(2,1)} %all_to_all.15.err_ref), channel_id=1, source_target_pairs={{0,1},{1,0},{2,3},{3,2},{4,5},{5,4},{6,7},{7,6},{8,9},{9,8},{10,11... | collective-permute-start | bytes 3145736 | tf_op jit(solution)/shard_map/ppermute | solution.py:21
  127.5 0.9 copy-start.3
  128.4 2.4 %copy-start.5 = (bf16[256,384]{0,1:T(8,128)(2,1)S(1)}, bf16[256,384]{0,1:T(8,128)(2,1)}, u32[]{:S(2)}) copy-start(bf16[256,384]{0,1:T(8,128)(2,1)} %copy-done.4) | copy-start | bytes 589828

commit v3 on v2

--- a/solution.py
+++ b/solution.py
@@ -52,6 +52,66 @@
         compiler_params=pltpu.CompilerParams(vmem_limit_bytes=32 * 1024 * 1024),
         cost_estimate=pl.CostEstimate(flops=flops, bytes_accessed=2_000_000, transcendentals=0),
     )
+
+
+def pack_kernel(enc_ref, bias_ref, dec_ref, out_ref, bias_buf, sems):
+    loads = [
+        pltpu.make_async_copy(dec_ref.at[0], out_ref.at[0:384], sems.at[0]),
+        pltpu.make_async_copy(dec_ref.at[1], out_ref.at[384:768], sems.at[1]),
+        pltpu.make_async_copy(enc_ref.at[0:512], out_ref.at[768:1280, 0:384], sems.at[2]),
+        pltpu.make_async_copy(enc_ref.at[512:1024], out_ref.at[768:1280, 384:768], sems.at[3]),
+    ]
+    bias_load = pltpu.make_async_copy(bias_ref, bias_buf, sems.at[4])
+    bias_load.start()
+    for load in loads:
+        load.start()
+    bias_load.wait()
+    rest = jnp.broadcast_to(bias_buf[...], (16, 384))
+    row = lax.broadcasted_iota(jnp.int32, (16, 384), 0)
+    rows = jnp.zeros((16, 384), F32)
+    for i in range(3):
+        piece = rest.astype(BF).astype(F32)
+        rows = jnp.where(row == i, piece, rows)
+        rest = rest - piece
+    out_ref[1280:1296, 0:384] = rows.astype(BF)
+    for load in loads:
+        load.wait()
+
+
+def pack(encoder, bias, decoder):
+    out = jax.ShapeDtypeStruct((1296, 1024), BF)
+    scratch = [pltpu.VMEM((1, 384), F32), pltpu.SemaphoreType.DMA((5,))]
+    encoder, bias, decoder = (pltpu.with_memory_space_constraint(a, pltpu.HBM) for a in (encoder, bias, decoder))
+    return call(pack_kernel, out, [ANYWHERE] * 3, VMEM, 1, scratch)(
+        encoder, bias, decoder
+    )
+
+
+def forward_kernel(rows_ref, own_ref, sib_ref, part_ref, lat_ref, other_ref):
+    def dot(a, b):
+        return jnp.dot(a, b, preferred_element_type=F32)
+
+    lats = []
+    for from_ref, to_ref in ((own_ref, lat_ref), (sib_ref, other_ref)):
+        pieces = from_ref[1280:1296, 0:384].astype(F32)
+        lat = dot(rows_ref[:, 0:512], from_ref[768:1280, 0:384])
+        lat += dot(rows_ref[:, 512:1024], from_ref[768:1280, 384:768])
+        lat += pieces[0:1] + pieces[1:2] + pieces[2:3]
+        lats.append(jnp.maximum(lat, 0.0).astype(BF))
+        to_ref[...] = lats[-1]
+    for s in range(2):
+        decoder = slice(384 * s, 384 * (s + 1))
+        total = dot(lats[0], own_ref[decoder, :]) + dot(lats[1], sib_ref[decoder, :])
+        part_ref[:, :, 1024 * s : 1024 * (s + 1)] = total.astype(BF).reshape(4, 64, 1024)
+
+
+def forward(rows, own, sibling):
+    outs = (
+        jax.ShapeDtypeStruct((4, 64, 2048), BF),
+        jax.ShapeDtypeStruct((256, 384), BF),
+        jax.ShapeDtypeStruct((256, 384), BF),
+    )
+    return call(forward_kernel, outs, [VMEM] * 3, (VMEM,) * 3, 1_207_959_552)(rows, own, sibling)
 
 
 def copies_kernel(own_ref, next_ref, out_ref):
@@ -119,34 +179,24 @@
 
 def per_device(residual, targets, enc_weight, enc_bias, dec_weight):
     w_encode = enc_weight[0]
-    bias_row = enc_bias[0]
     decoder = dec_weight[0]
     target = targets[0].astype(F32)
     latent = lax.axis_index("latent")
     z_at = (latent // 8) * 16
     row_set = (latent ^ (latent // 2) ^ (latent // 8)) & 1
 
+    packed = pack(w_encode, enc_bias, decoder)
+    sibling = swap_cores(packed)
+
     mine = lax.all_gather(residual[0], "latent", axis=0, tiled=True, axis_index_groups=ALONG_Z)
+    mine, sibling = lax.optimization_barrier((mine, sibling))
     mine = lax.all_gather(mine, "latent", axis=0, tiled=True, axis_index_groups=ALONG_Y)
-    other = swap_cores(mine)
-
-    def encode(rows):
-        pre = jnp.dot(rows, w_encode, preferred_element_type=F32) + bias_row
-        return jax.nn.relu(pre).astype(BF)
-
-    lat_mine = encode(mine)
-    lat_other = encode(other)
-
-    def decode(lat):
-        return jnp.concatenate(
-            [jnp.dot(lat, decoder[s], preferred_element_type=F32) for s in range(2)], axis=1
-        )
-
-    received = swap_cores(decode(lat_other).astype(BF))
-    part = (decode(lat_mine) + received.astype(F32)).astype(BF)
+    part, lat_mine, lat_sibling = forward(mine, packed, sibling)
+    lat_other = swap_cores(lat_sibling)
     part = lax.all_to_all(part, "latent", 0, 0, tiled=True, axis_index_groups=ALONG_Y)
-    part = jnp.sum(part.reshape(4, 64, 2048).astype(F32), axis=0)
+    part = jnp.sum(part.astype(F32), axis=0)
     shifted = shift_layer(part[:, 1024:].astype(BF), 1)
+    shifted, lat_t, other_t = lax.optimization_barrier((shifted, lat_mine.T, lat_other.T))
     part = part[:, :1024] + shifted.astype(F32)
     own = lax.dynamic_slice(part, (z_at, 0), (16, 1024)) - target
     part = lax.dynamic_update_slice(part, own, (z_at, 0))
@@ -159,8 +209,8 @@
     both = copies(error, after)
     mine_err = lax.all_to_all(both, "latent", 0, 0, tiled=True, axis_index_groups=ALONG_Y)
     other_err = swap_cores(mine_err)
-    parts, held = first_gradients(mine_err, lat_mine.T, decoder)
-    dec_grad, lat_grad = last_gradients(row_set, other_err, lat_other.T, decoder, parts, held)
+    parts, held = first_gradients(mine_err, lat_t, decoder)
+    dec_grad, lat_grad = last_gradients(row_set, other_err, other_t, decoder, parts, held)
     return recon[None], dec_grad[None], lat_grad[None]
 
 

time: 135 us -> 130 us (0.963)
  blocking collectives: 72.5 us -> 53.7 us
  waiting for transfers between devices: 32.2 us -> 44.9 us
  Pallas kernels: 4.34 us -> 8.83 us
  starting transfers between devices: 16.6 us -> 19.5 us
  matrix products: 2.75 us -> 0 us
    all_to_all x1 -> x0, blocking collectives: 19.2 us -> none  [per_device(): lax.all_to_all(part, 'latent', 0, 0, tiled=True, axis_index_groups=ALONG_Y)]
    all_to_all x0 -> x1, waiting for transfers between devices: none -> 13.5 us  [per_device(): lax.all_to_all(part, 'latent', 0, 0, tiled=True, axis_index_groups=ALONG_Y)]
    pallas_call x0 -> x2, Pallas kernels: none -> 4.49 us  [the longest x1 2.84 us: forward(): call(forward_kernel, outs, [VMEM] * 3, (VMEM,) * 3, 1207959552)]
    all_to_all x0 -> x1, starting transfers between devices: none -> 3.8 us  [per_device(): lax.all_to_all(part, 'latent', 0, 0, tiled=True, axis_index_groups=ALONG_Y)]
    dot_general x6 -> x0, matrix products: 2.75 us -> none  [the longest x4 1.82 us: decode(): jnp.dot(lat, decoder[s], preferred_element_type=F32)]
    unnamed x14 -> x6, local copies, waits for them, and re-layouts: 1.37 us -> 0.01 us
  transfers between devices with their start and end apart: 7 -> 8, of which waited for: 6 -> 6; matrix products, arithmetic and copies ran while one was open for 2% -> 1% of each run, Pallas kernels for 2% -> 2%
where the time goes in v3:
time: 130 us; the launch traced here: 129 us
  blocking collectives  53.7 us (41%)
  waiting for transfers between devices  44.9 us (35%)
  starting transfers between devices  19.5 us (15%)
  Pallas kernels  8.83 us (7%)
    all_gather x1, blocking collectives, per_device(): lax.all_gather(residual[0], 'latent', axis=0, tiled=True, axis_index_grou...  24.7 us
    ppermute x2, waiting for transfers between devices, exchange_z(): return lax.ppermute(block, 'latent', route)  21.6 us
    all_to_all x1, blocking collectives, per_device(): lax.all_to_all(both, 'latent', 0, 0, tiled=True, axis_index_groups=ALONG_Y)  16 us
    all_to_all x1, waiting for transfers between devices, per_device(): lax.all_to_all(part, 'latent', 0, 0, tiled=True, axis_index_groups=ALONG_Y)  13.5 us
    all_gather x1, blocking collectives, per_device(): lax.all_gather(mine, 'latent', axis=0, tiled=True, axis_index_groups=ALON...  12.9 us
    ppermute x2, waiting for transfers between devices, shift_layer(): return lax.ppermute(block, 'layer', route)  9.43 us
    ppermute x3, starting transfers between devices, swap_cores(): return lax.ppermute(block, 'latent', [(i, i ^ 1) for i in range(32)])  5.94 us
    ppermute x2, starting transfers between devices, shift_layer(): return lax.ppermute(block, 'layer', route)  5.58 us
  transfers between devices with their start and end apart: 8, of which 6 were waited for; matrix products, arithmetic and copies ran while one was open for 1% of the time, Pallas kernels for 2%

profile of v3, /device:TPU:6, one launch (start us, length us, event | category | flops | bytes accessed | tf_op | source)
XLA Modules:
  0.0 129.0 jit_solution(13597228934318840003)
XLA Ops:
  0.6 0.0 copy-start.2
  0.6 1.7 %shard_map.76.own_ref = bf16[1296,1024]{1,0:T(8,128)(2,1)S(1)} custom-call(bf16[1024,384]{1,0:T(8,128)(2,1)} %bitcast.18, f32[1,384]{1,0:T(1,128)} %bias_ref.1, bf16[2,384,1024]{2,1,0:T(8,128)(2,1)} %bitcast.13), custom_call_target="tpu_custom_call" | custom-call | flops 1 | bytes 2000000 | tf_op jit(solution)/shard_map/pallas_call | solution.py:85
  2.3 1.9 %collective-permute-start = (bf16[1296,1024]{1,0:T(8,128)(2,1)S(1)}, bf16[1296,1024]{1,0:T(8,128)(2,1)S(1)}, u32[]{:S(2)}, u32[]{:S(2)}) collective-permute-start(bf16[1296,1024]{1,0:T(8,128)(2,1)S(1)} %shard_map.76.own_ref), channel_id=1, source_target_pairs={{0,1},{1,0},{2,3},{3,2},{4,5},{5,4},{6,7},{7,6},{8,9},{9,8},{10,11... | collective-permute-start | bytes 7962632 | tf_op jit(solution)/shard_map/ppermute | solution.py:21
  4.2 0.0 copy-done.2
  4.2 24.7 %all-gather = bf16[1,64,1024]{2,1,0:T(8,128)(2,1)S(1)} all-gather(bf16[1,16,1024]{2,1,0:T(8,128)(2,1)S(1)} %copy-done.2), channel_id=2, replica_groups={{0,9,16,25},{1,8,17,24},{3,10,19,26},{2,11,18,27},{4,13,20,29},{5,12,21..., dimensions={1}, use_global_device_ids=true | all-gather | bytes 163840 | tf_op jit(solution)/shard_map/all_gather | solution.py:191
  29.0 0.0 collective-permute-done.sib_ref
  29.0 12.9 %all_gather.7.rows_ref = bf16[256,1024]{1,0:T(8,128)(2,1)S(1)} all-gather(bf16[64,1024]{1,0:T(8,128)(2,1)S(1)} %bitcast.19), channel_id=1, replica_groups={{0,3,4,7},{1,2,5,6},{9,10,13,14},{8,11,12,15},{16,19,20,23},{17,18,21,2..., dimensions={0}, use_global_device_ids=true | all-gather | bytes 655360 | tf_op jit(solution)/shard_map/all_gather | solution.py:193
  41.9 2.8 %shard_map.77 = (bf16[4,64,2048]{2,1,0:T(8,128)(2,1)}, bf16[256,384]{1,0:T(8,128)(2,1)S(1)}, bf16[256,384]{1,0:T(8,128)(2,1)S(1)}) custom-call(bf16[256,1024]{1,0:T(8,128)(2,1)S(1)} %all_gather.7.rows_ref, bf16[1296,1024]{1,0:T(8,128)(2,1)S(1)} %shard_map.76.own_ref, bf16[1296,1024]{1,0:T(8,128)(2,1)S(1)} %collective-permute-done.sib_ref), custom_call_target="tpu_custom_call" | custom-call | flops 1207959552 | bytes 2000000 | tf_op jit(solution)/shard_map/pallas_call | solution.py:114
  44.7 0.0 copy-start.1
  44.8 3.8 %all-to-all-start = ((bf16[4,64,2048]{2,1,0:T(8,128)(2,1)}), bf16[4,64,2048]{2,1,0:T(8,128)(2,1)S(1)}, u32[]{:S(2)}, u32[]{:S(2)}) async-start(bf16[4,64,2048]{2,1,0:T(8,128)(2,1)} %get-tuple-element.19), calls=%async_computation | async-start | bytes 2097152 | tf_op jit(solution)/shard_map/all_to_all | solution.py:196
  48.6 0.1 copy.9
  48.7 2.1 %collective-permute-start.2 = (bf16[256,384]{0,1:T(8,128)(2,1)S(1)}, bf16[256,384]{0,1:T(8,128)(2,1)S(1)}, u32[]{:S(2)}, u32[]{:S(2)}) collective-permute-start(bf16[256,384]{0,1:T(8,128)(2,1)S(1)} %copy.9), channel_id=1, source_target_pairs={{0,1},{1,0},{2,3},{3,2},{4,5},{5,4},{6,7},{7,6},{8,9},{9,8},{10,11... | collective-permute-start | bytes 589832 | tf_op jit(solution)/shard_map/ppermute | solution.py:21
  50.8 13.5 %all-to-all-done = bf16[4,64,2048]{2,1,0:T(8,128)(2,1)S(1)} async-done(((bf16[4,64,2048]{2,1,0:T(8,128)(2,1)}), bf16[4,64,2048]{2,1,0:T(8,128)(2,1)S(1)}, u32[]{:S(2)}, u32[]{:S(2)}) %all-to-all-start) | async-done | bytes 1048608 | tf_op jit(solution)/shard_map/all_to_all | solution.py:196
  64.3 0.2 convert_reduce_fusion
  64.5 2.8 %collective-permute-start.1 = (bf16[64,1024]{1,0:T(8,128)(2,1)S(1)}, bf16[64,1024]{1,0:T(8,128)(2,1)S(1)}, u32[]{:S(2)}, u32[]{:S(2)}) collective-permute-start(bf16[64,1024]{1,0:T(8,128)(2,1)S(1)} %slice.13), channel_id=1, source_target_pairs={{0,32},{32,64},{64,96},{96,128},{128,160},{160,192},{192,224},{224... | collective-permute-start | bytes 393224 | tf_op jit(solution)/shard_map/ppermute | solution.py:37
  67.4 0.1 copy.8
  67.5 0.0 collective-permute-done.2
  67.5 3.8 %collective-permute-done.1 = bf16[64,1024]{1,0:T(8,128)(2,1)S(1)} collective-permute-done((bf16[64,1024]{1,0:T(8,128)(2,1)S(1)}, bf16[64,1024]{1,0:T(8,128)(2,1)S(1)}, u32[]{:S(2)}, u32[]{:S(2)}) %collective-permute-start.1) | collective-permute-done | bytes 131104 | tf_op jit(solution)/shard_map/ppermute | solution.py:37
  71.4 0.0 copy-done.1
  71.4 0.0 copy-start
  71.4 2.3 %collective-permute-start.3 = (bf16[64,1024]{1,0:T(8,128)(2,1)S(1)}, bf16[64,1024]{1,0:T(8,128)(2,1)S(1)}, u32[]{:S(2)}, u32[]{:S(2)}) collective-permute-start(bf16[64,1024]{1,0:T(8,128)(2,1)S(1)} %convert_element_type.35), channel_id=1, source_target_pairs={{0,9},{1,24},{3,10},{2,27},{4,13},{5,28},{7,14},{6,31},{9,0},{8,17... | collective-permute-start | bytes 393224 | tf_op jit(solution)/shard_map/ppermute | solution.py:31
  73.7 12.0 %collective-permute-done.3 = bf16[64,1024]{1,0:T(8,128)(2,1)S(1)} collective-permute-done((bf16[64,1024]{1,0:T(8,128)(2,1)S(1)}, bf16[64,1024]{1,0:T(8,128)(2,1)S(1)}, u32[]{:S(2)}, u32[]{:S(2)}) %collective-permute-start.3) | collective-permute-done | bytes 131104 | tf_op jit(solution)/shard_map/ppermute | solution.py:31
  85.8 1.9 %collective-permute-start.4 = (bf16[64,1024]{1,0:T(8,128)(2,1)S(1)}, bf16[64,1024]{1,0:T(8,128)(2,1)S(1)}, u32[]{:S(2)}, u32[]{:S(2)}) collective-permute-start(bf16[64,1024]{1,0:T(8,128)(2,1)S(1)} %fusion), channel_id=1, source_target_pairs={{0,25},{1,8},{3,26},{2,11},{4,29},{5,12},{7,30},{6,15},{9,16},{8,1... | collective-permute-start | bytes 393224 | tf_op jit(solution)/shard_map/ppermute | solution.py:31
  87.7 9.6 %collective-permute-done.4 = bf16[64,1024]{1,0:T(8,128)(2,1)S(1)} collective-permute-done((bf16[64,1024]{1,0:T(8,128)(2,1)S(1)}, bf16[64,1024]{1,0:T(8,128)(2,1)S(1)}, u32[]{:S(2)}, u32[]{:S(2)}) %collective-permute-start.4) | collective-permute-done | bytes 131104 | tf_op jit(solution)/shard_map/ppermute | solution.py:31
  97.2 0.1 multiply_convert_fusion
  97.3 2.7 %collective-permute-start.5 = (bf16[64,1024]{1,0:T(8,128)(2,1)S(1)}, bf16[64,1024]{1,0:T(8,128)(2,1)S(1)}, u32[]{:S(2)}, u32[]{:S(2)}) collective-permute-start(bf16[64,1024]{1,0:T(8,128)(2,1)S(1)} %get-tuple-element.31.own_ref), channel_id=1, source_target_pairs={{32,0},{64,32},{96,64},{128,96},{160,128},{192,160},{224,192},{256... | collective-permute-start | bytes 393224 | tf_op jit(solution)/shard_map/ppermute | solution.py:37
  100.0 0.6 fusion.2
  100.7 5.6 %collective-permute-done.5.next_ref = bf16[64,1024]{1,0:T(8,128)(2,1)S(1)} collective-permute-done((bf16[64,1024]{1,0:T(8,128)(2,1)S(1)}, bf16[64,1024]{1,0:T(8,128)(2,1)S(1)}, u32[]{:S(2)}, u32[]{:S(2)}) %collective-permute-start.5) | collective-permute-done | bytes 131104 | tf_op jit(solution)/shard_map/ppermute | solution.py:37
  106.3 0.1 shard_map.78
  106.3 16.0 %all_to_all.10.err_ref = bf16[4,2,64,1024]{3,2,1,0:T(8,128)(2,1)} all-to-all(bf16[4,2,64,1024]{3,2,1,0:T(8,128)(2,1)S(1)} %shard_map.78), channel_id=1, replica_groups={{0,3,4,7},{1,2,5,6},{9,10,13,14},{8,11,12,15},{16,19,20,23},{17,18,21,2..., dimensions={0} | all-to-all | bytes 2097152 | tf_op jit(solution)/shard_map/all_to_all | solution.py:210
  122.3 1.9 %collective-permute-start.6 = (bf16[4,2,64,1024]{3,2,1,0:T(8,128)(2,1)}, bf16[4,2,64,1024]{3,2,1,0:T(8,128)(2,1)S(1)}, u32[]{:S(2)}, u32[]{:S(2)}) collective-permute-start(bf16[4,2,64,1024]{3,2,1,0:T(8,128)(2,1)} %all_to_all.10.err_ref), channel_id=1, source_target_pairs={{0,1},{1,0},{2,3},{3,2},{4,5},{5,4},{6,7},{7,6},{8,9},{9,8},{10,11... | collective-permute-start | bytes 3145736 | tf_op jit(solution)/shard_map/ppermute | solution.py:21
  124.3 0.0 copy-done
  124.3 2.3 %shard_map.79 = (f32[2,384,1024]{2,1,0:T(8,128)S(1)}, bf16[256,384]{1,0:T(8,128)(2,1)S(1)}) custom-call(bf16[4,2,64,1024]{3,2,1,0:T(8,128)(2,1)} %all_to_all.10.err_ref, bf16[384,256]{1,0:T(8,128)(2,1)S(1)} %bitcast.17, bf16[2,384,1024]{2,1,0:T(8,128)(2,1)S(1)} %bitcast.14), custom_call_target="tpu_custom_call" | custom-call | flops 805306368 | bytes 2000000 | tf_op jit(solution)/shard_map/pallas_call | solution.py:146
  126.6 0.5 collective-permute-done.6.err_ref
  127.1 1.9 %shard_map.80 = (bf16[2,384,1024]{2,1,0:T(8,128)(2,1)}, bf16[512,384]{1,0:T(8,128)(2,1)}) custom-call(s32[1]{0:T(128)} %bitcast.8.set_ref, bf16[4,2,64,1024]{3,2,1,0:T(8,128)(2,1)S(1)} %collective-permute-done.6.err_ref, bf16[384,256]{1,0:T(8,128)(2,1)S(1)} %bitcast.16, bf16[2,384,1024]{2,1,0:T(8,128)(2,1)S(1)} %bitcast.15, ...), custom_call_target="tpu_custom_call" | custom-call | flops 805306368 | bytes 2000000 | tf_op jit(solution)/shard_map/pallas_call | solution.py:175
  (5 shorter events, 0.1 us)
Async XLA Ops:
  0.6 3.6 %copy-start.2 = (bf16[1,16,1024]{2,1,0:T(8,128)(2,1)S(1)}, bf16[1,16,1024]{2,1,0:T(8,128)(2,1)}, u32[]{:S(2)}) copy-start(bf16[1,16,1024]{2,1,0:T(8,128)(2,1)} %param.5) | copy-start | bytes 98308
  2.3 26.7 %collective-permute-start = (bf16[1296,1024]{1,0:T(8,128)(2,1)S(1)}, bf16[1296,1024]{1,0:T(8,128)(2,1)S(1)}, u32[]{:S(2)}, u32[]{:S(2)}) collective-permute-start(bf16[1296,1024]{1,0:T(8,128)(2,1)S(1)} %shard_map.76.own_ref), channel_id=1, source_target_pairs={{0,1},{1,0},{2,3},{3,2},{4,5},{5,4},{6,7},{7,6},{8,9},{9,8},{10,11... | collective-permute-start | bytes 7962632 | tf_op jit(solution)/shard_map/ppermute | solution.py:21
  44.7 26.6 %copy-start.1 = (bf16[1,16,1024]{2,1,0:T(8,128)(2,1)S(1)}, bf16[1,16,1024]{2,1,0:T(8,128)(2,1)}, u32[]{:S(2)}) copy-start(bf16[1,16,1024]{2,1,0:T(8,128)(2,1)} %param.6) | copy-start | bytes 98308
  44.8 19.5 %all-to-all-start = ((bf16[4,64,2048]{2,1,0:T(8,128)(2,1)}), bf16[4,64,2048]{2,1,0:T(8,128)(2,1)S(1)}, u32[]{:S(2)}, u32[]{:S(2)}) async-start(bf16[4,64,2048]{2,1,0:T(8,128)(2,1)} %get-tuple-element.19), calls=%async_computation | async-start | bytes 2097152 | tf_op jit(solution)/shard_map/all_to_all | solution.py:196
  48.7 18.8 %collective-permute-start.2 = (bf16[256,384]{0,1:T(8,128)(2,1)S(1)}, bf16[256,384]{0,1:T(8,128)(2,1)S(1)}, u32[]{:S(2)}, u32[]{:S(2)}) collective-permute-start(bf16[256,384]{0,1:T(8,128)(2,1)S(1)} %copy.9), channel_id=1, source_target_pairs={{0,1},{1,0},{2,3},{3,2},{4,5},{5,4},{6,7},{7,6},{8,9},{9,8},{10,11... | collective-permute-start | bytes 589832 | tf_op jit(solution)/shard_map/ppermute | solution.py:21
  64.5 6.9 %collective-permute-start.1 = (bf16[64,1024]{1,0:T(8,128)(2,1)S(1)}, bf16[64,1024]{1,0:T(8,128)(2,1)S(1)}, u32[]{:S(2)}, u32[]{:S(2)}) collective-permute-start(bf16[64,1024]{1,0:T(8,128)(2,1)S(1)} %slice.13), channel_id=1, source_target_pairs={{0,32},{32,64},{64,96},{96,128},{128,160},{160,192},{192,224},{224... | collective-permute-start | bytes 393224 | tf_op jit(solution)/shard_map/ppermute | solution.py:37
  71.4 52.9 %copy-start = (bf16[1,2,384,1024]{3,2,1,0:T(8,128)(2,1)S(1)}, bf16[1,2,384,1024]{3,2,1,0:T(8,128)(2,1)}, u32[]{:S(2)}) copy-start(bf16[1,2,384,1024]{3,2,1,0:T(8,128)(2,1)} %param.9) | copy-start | bytes 4718596
  71.4 14.3 %collective-permute-start.3 = (bf16[64,1024]{1,0:T(8,128)(2,1)S(1)}, bf16[64,1024]{1,0:T(8,128)(2,1)S(1)}, u32[]{:S(2)}, u32[]{:S(2)}) collective-permute-start(bf16[64,1024]{1,0:T(8,128)(2,1)S(1)} %convert_element_type.35), channel_id=1, source_target_pairs={{0,9},{1,24},{3,10},{2,27},{4,13},{5,28},{7,14},{6,31},{9,0},{8,17... | collective-permute-start | bytes 393224 | tf_op jit(solution)/shard_map/ppermute | solution.py:31
  85.8 11.5 %collective-permute-start.4 = (bf16[64,1024]{1,0:T(8,128)(2,1)S(1)}, bf16[64,1024]{1,0:T(8,128)(2,1)S(1)}, u32[]{:S(2)}, u32[]{:S(2)}) collective-permute-start(bf16[64,1024]{1,0:T(8,128)(2,1)S(1)} %fusion), channel_id=1, source_target_pairs={{0,25},{1,8},{3,26},{2,11},{4,29},{5,12},{7,30},{6,15},{9,16},{8,1... | collective-permute-start | bytes 393224 | tf_op jit(solution)/shard_map/ppermute | solution.py:31
  97.3 9.0 %collective-permute-start.5 = (bf16[64,1024]{1,0:T(8,128)(2,1)S(1)}, bf16[64,1024]{1,0:T(8,128)(2,1)S(1)}, u32[]{:S(2)}, u32[]{:S(2)}) collective-permute-start(bf16[64,1024]{1,0:T(8,128)(2,1)S(1)} %get-tuple-element.31.own_ref), channel_id=1, source_target_pairs={{32,0},{64,32},{96,64},{128,96},{160,128},{192,160},{224,192},{256... | collective-permute-start | bytes 393224 | tf_op jit(solution)/shard_map/ppermute | solution.py:37
  122.3 4.8 %collective-permute-start.6 = (bf16[4,2,64,1024]{3,2,1,0:T(8,128)(2,1)}, bf16[4,2,64,1024]{3,2,1,0:T(8,128)(2,1)S(1)}, u32[]{:S(2)}, u32[]{:S(2)}) collective-permute-start(bf16[4,2,64,1024]{3,2,1,0:T(8,128)(2,1)} %all_to_all.10.err_ref), channel_id=1, source_target_pairs={{0,1},{1,0},{2,3},{3,2},{4,5},{5,4},{6,7},{7,6},{8,9},{9,8},{10,11... | collective-permute-start | bytes 3145736 | tf_op jit(solution)/shard_map/ppermute | solution.py:21

commit v4 on v3

--- a/solution.py
+++ b/solution.py
@@ -192,20 +192,22 @@
     mine, sibling = lax.optimization_barrier((mine, sibling))
     mine = lax.all_gather(mine, "latent", axis=0, tiled=True, axis_index_groups=ALONG_Y)
     part, lat_mine, lat_sibling = forward(mine, packed, sibling)
-    lat_other = swap_cores(lat_sibling)
     part = lax.all_to_all(part, "latent", 0, 0, tiled=True, axis_index_groups=ALONG_Y)
     part = jnp.sum(part.astype(F32), axis=0)
     shifted = shift_layer(part[:, 1024:].astype(BF), 1)
-    shifted, lat_t, other_t = lax.optimization_barrier((shifted, lat_mine.T, lat_other.T))
+    shifted, lat_t, lat_sibling = lax.optimization_barrier((shifted, lat_mine.T, lat_sibling))
     part = part[:, :1024] + shifted.astype(F32)
     own = lax.dynamic_slice(part, (z_at, 0), (16, 1024)) - target
     part = lax.dynamic_update_slice(part, own, (z_at, 0))
-    part = part + exchange_z(part.astype(BF), 1, 3).astype(F32)
+    halves = [swap_cores(lat_sibling[:128]), swap_cores(lat_sibling[128:])]
+    met, *halves = lax.optimization_barrier((exchange_z(part.astype(BF), 1, 3), *halves))
+    other_t = jnp.concatenate(halves).T
+    part = part + met.astype(F32)
     part = part + exchange_z(part.astype(BF), 3, 1).astype(F32)
     recon = (lax.dynamic_slice(part, (z_at, 0), (16, 1024)) + target).astype(BF)
 
     error = (0.25 * part).astype(BF)
-    after, recon = lax.optimization_barrier((shift_layer(error, -1), recon))
+    after, recon, other_t = lax.optimization_barrier((shift_layer(error, -1), recon, other_t))
     both = copies(error, after)
     mine_err = lax.all_to_all(both, "latent", 0, 0, tiled=True, axis_index_groups=ALONG_Y)
     other_err = swap_cores(mine_err)

time: 130 us -> 129 us (level)
  waiting for transfers between devices: 44.9 us -> 24.4 us
  blocking collectives: 53.7 us -> 72.9 us
    all_to_all x0 -> x1, blocking collectives: none -> 19.2 us  [per_device(): lax.all_to_all(part, 'latent', 0, 0, tiled=True, axis_index_groups=ALONG_Y)]
    all_to_all x1 -> x0, waiting for transfers between devices: 13.5 us -> none  [per_device(): lax.all_to_all(part, 'latent', 0, 0, tiled=True, axis_index_groups=ALONG_Y)]
    ppermute x2, waiting for transfers between devices: 21.6 us -> 13.8 us  [exchange_z(): return lax.ppermute(block, 'latent', route)]
    ppermute x3 -> x4, starting transfers between devices: 5.94 us -> 10 us  [swap_cores(): return lax.ppermute(block, 'latent', [(i, i ^ 1) for i in range(32)])]
    all_to_all x1 -> x0, starting transfers between devices: 3.8 us -> none  [per_device(): lax.all_to_all(part, 'latent', 0, 0, tiled=True, axis_index_groups=ALONG_Y)]
where the time goes in v4:
time: 129 us; the launch traced here: 128 us
  blocking collectives  72.9 us (57%)
  waiting for transfers between devices  24.4 us (19%)
  starting transfers between devices  20.2 us (16%)
  Pallas kernels  7.86 us (6%)
    all_gather x1, blocking collectives, per_device(): lax.all_gather(residual[0], 'latent', axis=0, tiled=True, axis_index_grou...  24.7 us
    all_to_all x1, blocking collectives, per_device(): lax.all_to_all(part, 'latent', 0, 0, tiled=True, axis_index_groups=ALONG_Y)  19.2 us
    all_to_all x1, blocking collectives, per_device(): lax.all_to_all(both, 'latent', 0, 0, tiled=True, axis_index_groups=ALONG_Y)  16 us
    ppermute x2, waiting for transfers between devices, exchange_z(): return lax.ppermute(block, 'latent', route)  13.8 us
    all_gather x1, blocking collectives, per_device(): lax.all_gather(mine, 'latent', axis=0, tiled=True, axis_index_groups=ALON...  12.9 us
    ppermute x4, starting transfers between devices, swap_cores(): return lax.ppermute(block, 'latent', [(i, i ^ 1) for i in range(32)])  10 us
    ppermute x2, waiting for transfers between devices, shift_layer(): return lax.ppermute(block, 'layer', route)  8.89 us
    ppermute x2, starting transfers between devices, shift_layer(): return lax.ppermute(block, 'layer', route)  6.12 us
  transfers between devices with their start and end apart: 8, of which 6 were waited for; matrix products, arithmetic and copies ran while one was open for 1% of the time, Pallas kernels for 2%

profile of v4, /device:TPU:6, one launch (start us, length us, event | category | flops | bytes accessed | tf_op | source)
XLA Modules:
  0.0 127.6 jit_solution(1250621307747448493)
XLA Ops:
  0.6 0.0 copy-start.2
  0.6 1.7 %shard_map.76.own_ref = bf16[1296,1024]{1,0:T(8,128)(2,1)S(1)} custom-call(bf16[1024,384]{1,0:T(8,128)(2,1)} %bitcast.18, f32[1,384]{1,0:T(1,128)} %bias_ref.1, bf16[2,384,1024]{2,1,0:T(8,128)(2,1)} %bitcast.14), custom_call_target="tpu_custom_call" | custom-call | flops 1 | bytes 2000000 | tf_op jit(solution)/shard_map/pallas_call | solution.py:85
  2.3 1.9 %collective-permute-start = (bf16[1296,1024]{1,0:T(8,128)(2,1)S(1)}, bf16[1296,1024]{1,0:T(8,128)(2,1)S(1)}, u32[]{:S(2)}, u32[]{:S(2)}) collective-permute-start(bf16[1296,1024]{1,0:T(8,128)(2,1)S(1)} %shard_map.76.own_ref), channel_id=1, source_target_pairs={{0,1},{1,0},{2,3},{3,2},{4,5},{5,4},{6,7},{7,6},{8,9},{9,8},{10,11... | collective-permute-start | bytes 7962632 | tf_op jit(solution)/shard_map/ppermute | solution.py:21
  4.2 0.0 copy-done.2
  4.2 24.7 %all-gather = bf16[1,64,1024]{2,1,0:T(8,128)(2,1)S(1)} all-gather(bf16[1,16,1024]{2,1,0:T(8,128)(2,1)S(1)} %copy-done.2), channel_id=2, replica_groups={{0,9,16,25},{1,8,17,24},{3,10,19,26},{2,11,18,27},{4,13,20,29},{5,12,21..., dimensions={1}, use_global_device_ids=true | all-gather | bytes 163840 | tf_op jit(solution)/shard_map/all_gather | solution.py:191
  29.0 0.0 collective-permute-done.sib_ref
  29.0 12.9 %all_gather.7.rows_ref = bf16[256,1024]{1,0:T(8,128)(2,1)S(1)} all-gather(bf16[64,1024]{1,0:T(8,128)(2,1)S(1)} %bitcast.19), channel_id=1, replica_groups={{0,3,4,7},{1,2,5,6},{9,10,13,14},{8,11,12,15},{16,19,20,23},{17,18,21,2..., dimensions={0}, use_global_device_ids=true | all-gather | bytes 655360 | tf_op jit(solution)/shard_map/all_gather | solution.py:193
  41.9 1.9 %shard_map.77 = (bf16[4,64,2048]{2,1,0:T(8,128)(2,1)S(1)}, bf16[256,384]{1,0:T(8,128)(2,1)S(1)}, bf16[256,384]{1,0:T(8,128)(2,1)S(1)}) custom-call(bf16[256,1024]{1,0:T(8,128)(2,1)S(1)} %all_gather.7.rows_ref, bf16[1296,1024]{1,0:T(8,128)(2,1)S(1)} %shard_map.76.own_ref, bf16[1296,1024]{1,0:T(8,128)(2,1)S(1)} %collective-permute-done.sib_ref), custom_call_target="tpu_custom_call" | custom-call | flops 1207959552 | bytes 2000000 | tf_op jit(solution)/shard_map/pallas_call | solution.py:114
  43.8 0.0 copy-start.1
  43.8 19.2 %all_to_all.10 = bf16[4,64,2048]{2,1,0:T(8,128)(2,1)S(1)} all-to-all(bf16[4,64,2048]{2,1,0:T(8,128)(2,1)S(1)} %get-tuple-element.23), channel_id=1, replica_groups={{0,3,4,7},{1,2,5,6},{9,10,13,14},{8,11,12,15},{16,19,20,23},{17,18,21,2..., dimensions={0} | all-to-all | bytes 2097152 | tf_op jit(solution)/shard_map/all_to_all | solution.py:195
  63.0 0.2 convert_reduce_fusion
  63.2 2.8 %collective-permute-start.1 = (bf16[64,1024]{1,0:T(8,128)(2,1)S(1)}, bf16[64,1024]{1,0:T(8,128)(2,1)S(1)}, u32[]{:S(2)}, u32[]{:S(2)}) collective-permute-start(bf16[64,1024]{1,0:T(8,128)(2,1)S(1)} %slice.23), channel_id=1, source_target_pairs={{0,32},{32,64},{64,96},{96,128},{128,160},{160,192},{192,224},{224... | collective-permute-start | bytes 393224 | tf_op jit(solution)/shard_map/ppermute | solution.py:37
  66.1 0.1 copy.8
  66.2 3.8 %collective-permute-done.1 = bf16[64,1024]{1,0:T(8,128)(2,1)S(1)} collective-permute-done((bf16[64,1024]{1,0:T(8,128)(2,1)S(1)}, bf16[64,1024]{1,0:T(8,128)(2,1)S(1)}, u32[]{:S(2)}, u32[]{:S(2)}) %collective-permute-start.1) | collective-permute-done | bytes 131104 | tf_op jit(solution)/shard_map/ppermute | solution.py:37
  70.1 0.0 copy-done.1
  70.2 2.2 %collective-permute-start.2 = (bf16[64,1024]{1,0:T(8,128)(2,1)S(1)}, bf16[64,1024]{1,0:T(8,128)(2,1)S(1)}, u32[]{:S(2)}, u32[]{:S(2)}) collective-permute-start(bf16[64,1024]{1,0:T(8,128)(2,1)S(1)} %convert_element_type.35), channel_id=1, source_target_pairs={{0,9},{1,24},{3,10},{2,27},{4,13},{5,28},{7,14},{6,31},{9,0},{8,17... | collective-permute-start | bytes 393224 | tf_op jit(solution)/shard_map/ppermute | solution.py:31
  72.3 0.1 copy.9
  72.5 4.2 %collective-permute-start.3 = (bf16[128,384]{0,1:T(8,128)(2,1)S(1)}, bf16[128,384]{0,1:T(8,128)(2,1)S(1)}, u32[]{:S(2)}, u32[]{:S(2)}) collective-permute-start(bf16[128,384]{0,1:T(8,128)(2,1)S(1)} %get-tuple-element.42), channel_id=1, source_target_pairs={{0,1},{1,0},{2,3},{3,2},{4,5},{5,4},{6,7},{7,6},{8,9},{9,8},{10,11... | collective-permute-start | bytes 294920 | tf_op jit(solution)/shard_map/ppermute | solution.py:21
  76.7 0.0 copy-start
  76.7 2.1 %collective-permute-start.4 = (bf16[128,384]{0,1:T(8,128)(2,1)S(1)}, bf16[128,384]{0,1:T(8,128)(2,1)S(1)}, u32[]{:S(2)}, u32[]{:S(2)}) collective-permute-start(bf16[128,384]{0,1:T(8,128)(2,1)S(1)} %get-tuple-element.41), channel_id=1, source_target_pairs={{0,1},{1,0},{2,3},{3,2},{4,5},{5,4},{6,7},{7,6},{8,9},{9,8},{10,11... | collective-permute-start | bytes 294920 | tf_op jit(solution)/shard_map/ppermute | solution.py:21
  78.7 0.0 collective-permute-done.3
  78.7 1.3 collective-permute-done.4
  80.0 4.3 %collective-permute-done.2 = bf16[64,1024]{1,0:T(8,128)(2,1)S(1)} collective-permute-done((bf16[64,1024]{1,0:T(8,128)(2,1)S(1)}, bf16[64,1024]{1,0:T(8,128)(2,1)S(1)}, u32[]{:S(2)}, u32[]{:S(2)}) %collective-permute-start.2) | collective-permute-done | bytes 131104 | tf_op jit(solution)/shard_map/ppermute | solution.py:31
  84.3 1.9 %collective-permute-start.5 = (bf16[64,1024]{1,0:T(8,128)(2,1)S(1)}, bf16[64,1024]{1,0:T(8,128)(2,1)S(1)}, u32[]{:S(2)}, u32[]{:S(2)}) collective-permute-start(bf16[64,1024]{1,0:T(8,128)(2,1)S(1)} %fusion), channel_id=1, source_target_pairs={{0,25},{1,8},{3,26},{2,11},{4,29},{5,12},{7,30},{6,15},{9,16},{8,1... | collective-permute-start | bytes 393224 | tf_op jit(solution)/shard_map/ppermute | solution.py:31
  86.3 9.5 %collective-permute-done.5 = bf16[64,1024]{1,0:T(8,128)(2,1)S(1)} collective-permute-done((bf16[64,1024]{1,0:T(8,128)(2,1)S(1)}, bf16[64,1024]{1,0:T(8,128)(2,1)S(1)}, u32[]{:S(2)}, u32[]{:S(2)}) %collective-permute-start.5) | collective-permute-done | bytes 131104 | tf_op jit(solution)/shard_map/ppermute | solution.py:31
  95.8 0.1 multiply_convert_fusion
  95.9 3.3 %collective-permute-start.6 = (bf16[64,1024]{1,0:T(8,128)(2,1)S(1)}, bf16[64,1024]{1,0:T(8,128)(2,1)S(1)}, u32[]{:S(2)}, u32[]{:S(2)}) collective-permute-start(bf16[64,1024]{1,0:T(8,128)(2,1)S(1)} %get-tuple-element.39.own_ref), channel_id=1, source_target_pairs={{32,0},{64,32},{96,64},{128,96},{160,128},{192,160},{224,192},{256... | collective-permute-start | bytes 393224 | tf_op jit(solution)/shard_map/ppermute | solution.py:37
  99.2 0.6 fusion.2
  99.8 5.1 %collective-permute-done.6.next_ref = bf16[64,1024]{1,0:T(8,128)(2,1)S(1)} collective-permute-done((bf16[64,1024]{1,0:T(8,128)(2,1)S(1)}, bf16[64,1024]{1,0:T(8,128)(2,1)S(1)}, u32[]{:S(2)}, u32[]{:S(2)}) %collective-permute-start.6) | collective-permute-done | bytes 131104 | tf_op jit(solution)/shard_map/ppermute | solution.py:37
  104.8 0.1 shard_map.78
  104.9 16.0 %all_to_all.11.err_ref = bf16[4,2,64,1024]{3,2,1,0:T(8,128)(2,1)} all-to-all(bf16[4,2,64,1024]{3,2,1,0:T(8,128)(2,1)S(1)} %shard_map.78), channel_id=1, replica_groups={{0,3,4,7},{1,2,5,6},{9,10,13,14},{8,11,12,15},{16,19,20,23},{17,18,21,2..., dimensions={0} | all-to-all | bytes 2097152 | tf_op jit(solution)/shard_map/all_to_all | solution.py:212
  120.9 1.9 %collective-permute-start.7 = (bf16[4,2,64,1024]{3,2,1,0:T(8,128)(2,1)}, bf16[4,2,64,1024]{3,2,1,0:T(8,128)(2,1)S(1)}, u32[]{:S(2)}, u32[]{:S(2)}) collective-permute-start(bf16[4,2,64,1024]{3,2,1,0:T(8,128)(2,1)} %all_to_all.11.err_ref), channel_id=1, source_target_pairs={{0,1},{1,0},{2,3},{3,2},{4,5},{5,4},{6,7},{7,6},{8,9},{9,8},{10,11... | collective-permute-start | bytes 3145736 | tf_op jit(solution)/shard_map/ppermute | solution.py:21
  122.8 0.0 copy-done
  122.8 2.3 %shard_map.79 = (f32[2,384,1024]{2,1,0:T(8,128)S(1)}, bf16[256,384]{1,0:T(8,128)(2,1)S(1)}) custom-call(bf16[4,2,64,1024]{3,2,1,0:T(8,128)(2,1)} %all_to_all.11.err_ref, bf16[384,256]{1,0:T(8,128)(2,1)S(1)} %bitcast.17, bf16[2,384,1024]{2,1,0:T(8,128)(2,1)S(1)} %bitcast.15), custom_call_target="tpu_custom_call" | custom-call | flops 805306368 | bytes 2000000 | tf_op jit(solution)/shard_map/pallas_call | solution.py:146
  125.2 0.5 collective-permute-done.7.err_ref
  125.6 1.9 %shard_map.80 = (bf16[2,384,1024]{2,1,0:T(8,128)(2,1)}, bf16[512,384]{1,0:T(8,128)(2,1)}) custom-call(s32[1]{0:T(128)} %bitcast.8.set_ref, bf16[4,2,64,1024]{3,2,1,0:T(8,128)(2,1)S(1)} %collective-permute-done.7.err_ref, bf16[384,256]{1,0:T(8,128)(2,1)S(1)} %maximum_bitcast_fusion.lat_ref, bf16[2,384,1024]{2,1,0:T(8,128)(2,1)S(1)} %bitcast.16, ...), custom_call_target="tpu_custom_call" | custom-call | flops 805306368 | bytes 2000000 | tf_op jit(solution)/shard_map/pallas_call | solution.py:175
  (7 shorter events, 0.1 us)
Async XLA Ops:
  0.6 3.6 %copy-start.2 = (bf16[1,16,1024]{2,1,0:T(8,128)(2,1)S(1)}, bf16[1,16,1024]{2,1,0:T(8,128)(2,1)}, u32[]{:S(2)}) copy-start(bf16[1,16,1024]{2,1,0:T(8,128)(2,1)} %param.5) | copy-start | bytes 98308
  2.3 26.7 %collective-permute-start = (bf16[1296,1024]{1,0:T(8,128)(2,1)S(1)}, bf16[1296,1024]{1,0:T(8,128)(2,1)S(1)}, u32[]{:S(2)}, u32[]{:S(2)}) collective-permute-start(bf16[1296,1024]{1,0:T(8,128)(2,1)S(1)} %shard_map.76.own_ref), channel_id=1, source_target_pairs={{0,1},{1,0},{2,3},{3,2},{4,5},{5,4},{6,7},{7,6},{8,9},{9,8},{10,11... | collective-permute-start | bytes 7962632 | tf_op jit(solution)/shard_map/ppermute | solution.py:21
  43.8 26.3 %copy-start.1 = (bf16[1,16,1024]{2,1,0:T(8,128)(2,1)S(1)}, bf16[1,16,1024]{2,1,0:T(8,128)(2,1)}, u32[]{:S(2)}) copy-start(bf16[1,16,1024]{2,1,0:T(8,128)(2,1)} %param.6) | copy-start | bytes 98308
  63.2 6.9 %collective-permute-start.1 = (bf16[64,1024]{1,0:T(8,128)(2,1)S(1)}, bf16[64,1024]{1,0:T(8,128)(2,1)S(1)}, u32[]{:S(2)}, u32[]{:S(2)}) collective-permute-start(bf16[64,1024]{1,0:T(8,128)(2,1)S(1)} %slice.23), channel_id=1, source_target_pairs={{0,32},{32,64},{64,96},{96,128},{128,160},{160,192},{192,224},{224... | collective-permute-start | bytes 393224 | tf_op jit(solution)/shard_map/ppermute | solution.py:37
  70.2 14.1 %collective-permute-start.2 = (bf16[64,1024]{1,0:T(8,128)(2,1)S(1)}, bf16[64,1024]{1,0:T(8,128)(2,1)S(1)}, u32[]{:S(2)}, u32[]{:S(2)}) collective-permute-start(bf16[64,1024]{1,0:T(8,128)(2,1)S(1)} %convert_element_type.35), channel_id=1, source_target_pairs={{0,9},{1,24},{3,10},{2,27},{4,13},{5,28},{7,14},{6,31},{9,0},{8,17... | collective-permute-start | bytes 393224 | tf_op jit(solution)/shard_map/ppermute | solution.py:31
  72.5 6.2 %collective-permute-start.3 = (bf16[128,384]{0,1:T(8,128)(2,1)S(1)}, bf16[128,384]{0,1:T(8,128)(2,1)S(1)}, u32[]{:S(2)}, u32[]{:S(2)}) collective-permute-start(bf16[128,384]{0,1:T(8,128)(2,1)S(1)} %get-tuple-element.42), channel_id=1, source_target_pairs={{0,1},{1,0},{2,3},{3,2},{4,5},{5,4},{6,7},{7,6},{8,9},{9,8},{10,11... | collective-permute-start | bytes 294920 | tf_op jit(solution)/shard_map/ppermute | solution.py:21
  76.7 46.2 %copy-start = (bf16[1,2,384,1024]{3,2,1,0:T(8,128)(2,1)S(1)}, bf16[1,2,384,1024]{3,2,1,0:T(8,128)(2,1)}, u32[]{:S(2)}) copy-start(bf16[1,2,384,1024]{3,2,1,0:T(8,128)(2,1)} %param.9) | copy-start | bytes 4718596
  76.7 3.3 %collective-permute-start.4 = (bf16[128,384]{0,1:T(8,128)(2,1)S(1)}, bf16[128,384]{0,1:T(8,128)(2,1)S(1)}, u32[]{:S(2)}, u32[]{:S(2)}) collective-permute-start(bf16[128,384]{0,1:T(8,128)(2,1)S(1)} %get-tuple-element.41), channel_id=1, source_target_pairs={{0,1},{1,0},{2,3},{3,2},{4,5},{5,4},{6,7},{7,6},{8,9},{9,8},{10,11... | collective-permute-start | bytes 294920 | tf_op jit(solution)/shard_map/ppermute | solution.py:21
  84.3 11.5 %collective-permute-start.5 = (bf16[64,1024]{1,0:T(8,128)(2,1)S(1)}, bf16[64,1024]{1,0:T(8,128)(2,1)S(1)}, u32[]{:S(2)}, u32[]{:S(2)}) collective-permute-start(bf16[64,1024]{1,0:T(8,128)(2,1)S(1)} %fusion), channel_id=1, source_target_pairs={{0,25},{1,8},{3,26},{2,11},{4,29},{5,12},{7,30},{6,15},{9,16},{8,1... | collective-permute-start | bytes 393224 | tf_op jit(solution)/shard_map/ppermute | solution.py:31
  95.9 9.0 %collective-permute-start.6 = (bf16[64,1024]{1,0:T(8,128)(2,1)S(1)}, bf16[64,1024]{1,0:T(8,128)(2,1)S(1)}, u32[]{:S(2)}, u32[]{:S(2)}) collective-permute-start(bf16[64,1024]{1,0:T(8,128)(2,1)S(1)} %get-tuple-element.39.own_ref), channel_id=1, source_target_pairs={{32,0},{64,32},{96,64},{128,96},{160,128},{192,160},{224,192},{256... | collective-permute-start | bytes 393224 | tf_op jit(solution)/shard_map/ppermute | solution.py:37
  120.9 4.8 %collective-permute-start.7 = (bf16[4,2,64,1024]{3,2,1,0:T(8,128)(2,1)}, bf16[4,2,64,1024]{3,2,1,0:T(8,128)(2,1)S(1)}, u32[]{:S(2)}, u32[]{:S(2)}) collective-permute-start(bf16[4,2,64,1024]{3,2,1,0:T(8,128)(2,1)} %all_to_all.11.err_ref), channel_id=1, source_target_pairs={{0,1},{1,0},{2,3},{3,2},{4,5},{5,4},{6,7},{7,6},{8,9},{9,8},{10,11... | collective-permute-start | bytes 3145736 | tf_op jit(solution)/shard_map/ppermute | solution.py:21

commit v5 on v4

--- a/solution.py
+++ b/solution.py
@@ -55,13 +55,14 @@
 
 
 def pack_kernel(enc_ref, bias_ref, dec_ref, out_ref, bias_buf, sems):
-    loads = [
-        pltpu.make_async_copy(dec_ref.at[0], out_ref.at[0:384], sems.at[0]),
-        pltpu.make_async_copy(dec_ref.at[1], out_ref.at[384:768], sems.at[1]),
-        pltpu.make_async_copy(enc_ref.at[0:512], out_ref.at[768:1280, 0:384], sems.at[2]),
-        pltpu.make_async_copy(enc_ref.at[512:1024], out_ref.at[768:1280, 384:768], sems.at[3]),
-    ]
-    bias_load = pltpu.make_async_copy(bias_ref, bias_buf, sems.at[4])
+    pairs = [(dec_ref.at[i, pl.ds(j, 128)], out_ref.at[pl.ds(384 * i + j, 128)]) for i in range(2) for j in (0, 128, 256)]
+    pairs += [
+        (enc_ref.at[pl.ds(512 * i + j, 256)], out_ref.at[pl.ds(768 + j, 256), pl.ds(384 * i, 384)])
+        for i in range(2)
+        for j in (0, 256)
+    ]
+    loads = [pltpu.make_async_copy(pair[0], pair[1], sems.at[i]) for i, pair in enumerate(pairs)]
+    bias_load = pltpu.make_async_copy(bias_ref, bias_buf, sems.at[10])
     bias_load.start()
     for load in loads:
         load.start()
@@ -80,7 +81,7 @@
 
 def pack(encoder, bias, decoder):
     out = jax.ShapeDtypeStruct((1296, 1024), BF)
-    scratch = [pltpu.VMEM((1, 384), F32), pltpu.SemaphoreType.DMA((5,))]
+    scratch = [pltpu.VMEM((1, 384), F32), pltpu.SemaphoreType.DMA((11,))]
     encoder, bias, decoder = (pltpu.with_memory_space_constraint(a, pltpu.HBM) for a in (encoder, bias, decoder))
     return call(pack_kernel, out, [ANYWHERE] * 3, VMEM, 1, scratch)(
         encoder, bias, decoder
@@ -148,22 +149,33 @@
 
 def last_kernel(set_ref, err_ref, lat_ref, dec_ref, parts_ref, held_ref, dec_out, lat_out, dec_buf, lat_buf, sems):
     even = set_ref[0] * 16
-    sends = [pltpu.make_async_copy(dec_buf.at[s], dec_out.at[s], sems.at[s]) for s in range(2)]
-    sends.append(pltpu.make_async_copy(lat_buf, lat_out, sems.at[2]))
+    sends = [
+        pltpu.make_async_copy(
+            dec_buf.at[s, pl.ds(128 * i, 128)], dec_out.at[s, pl.ds(128 * i, 128)], sems.at[3 * s + i]
+        )
+        for s in range(2)
+        for i in range(3)
+    ]
+    sends += [
+        pltpu.make_async_copy(lat_buf.at[pl.ds(256 * i, 256)], lat_out.at[pl.ds(256 * i, 256)], sems.at[6 + i])
+        for i in range(2)
+    ]
     for s in range(2):
         total = parts_ref[s] + jnp.dot(lat_ref[...], rows_of(err_ref, s), preferred_element_type=F32)
         dec_buf[s] = total.astype(BF)
-        sends[s].start()
+        for i in range(3):
+            sends[3 * s + i].start()
     total = latent_rows(err_ref, dec_ref)
-    for y in range(4):
-        for z in range(4):
+    for z in range(4):
+        for y in range(4):
             here = y * 64 + z * 16
             there = z * 128 + y * 32
             at = even if (y ^ z) & 1 == 0 else 16 - even
             away = 16 - at
             lat_buf[pl.ds(pl.multiple_of(there + at, 16), 16), :] = held_ref[here : here + 16, :]
             lat_buf[pl.ds(pl.multiple_of(there + away, 16), 16), :] = total[here : here + 16, :]
-    sends[2].start()
+        if z % 2:
+            sends[6 + z // 2].start()
     for send in sends:
         send.wait()
 
@@ -171,7 +183,7 @@
 def last_gradients(row_set, err, lat_t, decoder, parts, held):
     outs = (jax.ShapeDtypeStruct((2, 384, 1024), BF), jax.ShapeDtypeStruct((512, 384), BF))
     specs = [pl.BlockSpec(memory_space=pltpu.SMEM)] + [VMEM] * 5
-    scratch = [pltpu.VMEM((2, 384, 1024), BF), pltpu.VMEM((512, 384), BF), pltpu.SemaphoreType.DMA((3,))]
+    scratch = [pltpu.VMEM((2, 384, 1024), BF), pltpu.VMEM((512, 384), BF), pltpu.SemaphoreType.DMA((8,))]
     return call(last_kernel, outs, specs, (ANYWHERE, ANYWHERE), 805_306_368, scratch)(
         row_set.reshape(1), err, lat_t, decoder, parts, held
     )

time: 129 us -> 129 us (level)
  no operation moved by 1% of the time
where the time goes in v5:
time: 129 us; the launch traced here: 128 us
  blocking collectives  72.9 us (57%)
  waiting for transfers between devices  25 us (19%)
  starting transfers between devices  19.7 us (15%)
  Pallas kernels  7.94 us (6%)
    all_gather x1, blocking collectives, per_device(): lax.all_gather(residual[0], 'latent', axis=0, tiled=True, axis_index_grou...  24.7 us
    all_to_all x1, blocking collectives, per_device(): lax.all_to_all(part, 'latent', 0, 0, tiled=True, axis_index_groups=ALONG_Y)  19.2 us
    all_to_all x1, blocking collectives, per_device(): lax.all_to_all(both, 'latent', 0, 0, tiled=True, axis_index_groups=ALONG_Y)  16 us
    ppermute x2, waiting for transfers between devices, exchange_z(): return lax.ppermute(block, 'latent', route)  13.8 us
    all_gather x1, blocking collectives, per_device(): lax.all_gather(mine, 'latent', axis=0, tiled=True, axis_index_groups=ALON...  12.9 us
    ppermute x4, starting transfers between devices, swap_cores(): return lax.ppermute(block, 'latent', [(i, i ^ 1) for i in range(32)])  10 us
    ppermute x2, waiting for transfers between devices, shift_layer(): return lax.ppermute(block, 'layer', route)  9.45 us
    ppermute x2, starting transfers between devices, shift_layer(): return lax.ppermute(block, 'layer', route)  5.56 us
  transfers between devices with their start and end apart: 8, of which 6 were waited for; matrix products, arithmetic and copies ran while one was open for 1% of the time, Pallas kernels for 2%

profile of v5, /device:TPU:6, one launch (start us, length us, event | category | flops | bytes accessed | tf_op | source)
XLA Modules:
  0.0 127.6 jit_solution(17233314949347238973)
XLA Ops:
  0.6 0.0 copy-start.2
  0.6 1.7 %shard_map.76.own_ref = bf16[1296,1024]{1,0:T(8,128)(2,1)S(1)} custom-call(bf16[1024,384]{1,0:T(8,128)(2,1)} %bitcast.18, f32[1,384]{1,0:T(1,128)} %bias_ref.1, bf16[2,384,1024]{2,1,0:T(8,128)(2,1)} %bitcast.14), custom_call_target="tpu_custom_call" | custom-call | flops 1 | bytes 2000000 | tf_op jit(solution)/shard_map/pallas_call | solution.py:86
  2.3 1.9 %collective-permute-start = (bf16[1296,1024]{1,0:T(8,128)(2,1)S(1)}, bf16[1296,1024]{1,0:T(8,128)(2,1)S(1)}, u32[]{:S(2)}, u32[]{:S(2)}) collective-permute-start(bf16[1296,1024]{1,0:T(8,128)(2,1)S(1)} %shard_map.76.own_ref), channel_id=1, source_target_pairs={{0,1},{1,0},{2,3},{3,2},{4,5},{5,4},{6,7},{7,6},{8,9},{9,8},{10,11... | collective-permute-start | bytes 7962632 | tf_op jit(solution)/shard_map/ppermute | solution.py:21
  4.3 0.0 copy-done.2
  4.3 24.7 %all-gather = bf16[1,64,1024]{2,1,0:T(8,128)(2,1)S(1)} all-gather(bf16[1,16,1024]{2,1,0:T(8,128)(2,1)S(1)} %copy-done.2), channel_id=2, replica_groups={{0,9,16,25},{1,8,17,24},{3,10,19,26},{2,11,18,27},{4,13,20,29},{5,12,21..., dimensions={1}, use_global_device_ids=true | all-gather | bytes 163840 | tf_op jit(solution)/shard_map/all_gather | solution.py:203
  29.0 0.0 collective-permute-done.sib_ref
  29.0 12.9 %all_gather.7.rows_ref = bf16[256,1024]{1,0:T(8,128)(2,1)S(1)} all-gather(bf16[64,1024]{1,0:T(8,128)(2,1)S(1)} %bitcast.19), channel_id=1, replica_groups={{0,3,4,7},{1,2,5,6},{9,10,13,14},{8,11,12,15},{16,19,20,23},{17,18,21,2..., dimensions={0}, use_global_device_ids=true | all-gather | bytes 655360 | tf_op jit(solution)/shard_map/all_gather | solution.py:205
  42.0 1.9 %shard_map.77 = (bf16[4,64,2048]{2,1,0:T(8,128)(2,1)S(1)}, bf16[256,384]{1,0:T(8,128)(2,1)S(1)}, bf16[256,384]{1,0:T(8,128)(2,1)S(1)}) custom-call(bf16[256,1024]{1,0:T(8,128)(2,1)S(1)} %all_gather.7.rows_ref, bf16[1296,1024]{1,0:T(8,128)(2,1)S(1)} %shard_map.76.own_ref, bf16[1296,1024]{1,0:T(8,128)(2,1)S(1)} %collective-permute-done.sib_ref), custom_call_target="tpu_custom_call" | custom-call | flops 1207959552 | bytes 2000000 | tf_op jit(solution)/shard_map/pallas_call | solution.py:115
  43.8 0.0 copy-start.1
  43.8 19.2 %all_to_all.10 = bf16[4,64,2048]{2,1,0:T(8,128)(2,1)S(1)} all-to-all(bf16[4,64,2048]{2,1,0:T(8,128)(2,1)S(1)} %get-tuple-element.23), channel_id=1, replica_groups={{0,3,4,7},{1,2,5,6},{9,10,13,14},{8,11,12,15},{16,19,20,23},{17,18,21,2..., dimensions={0} | all-to-all | bytes 2097152 | tf_op jit(solution)/shard_map/all_to_all | solution.py:207
  63.1 0.2 convert_reduce_fusion
  63.2 2.8 %collective-permute-start.1 = (bf16[64,1024]{1,0:T(8,128)(2,1)S(1)}, bf16[64,1024]{1,0:T(8,128)(2,1)S(1)}, u32[]{:S(2)}, u32[]{:S(2)}) collective-permute-start(bf16[64,1024]{1,0:T(8,128)(2,1)S(1)} %slice.23), channel_id=1, source_target_pairs={{0,32},{32,64},{64,96},{96,128},{128,160},{160,192},{192,224},{224... | collective-permute-start | bytes 393224 | tf_op jit(solution)/shard_map/ppermute | solution.py:37
  66.1 0.1 copy.8
  66.3 3.8 %collective-permute-done.1 = bf16[64,1024]{1,0:T(8,128)(2,1)S(1)} collective-permute-done((bf16[64,1024]{1,0:T(8,128)(2,1)S(1)}, bf16[64,1024]{1,0:T(8,128)(2,1)S(1)}, u32[]{:S(2)}, u32[]{:S(2)}) %collective-permute-start.1) | collective-permute-done | bytes 131104 | tf_op jit(solution)/shard_map/ppermute | solution.py:37
  70.1 0.0 copy-done.1
  70.2 2.2 %collective-permute-start.2 = (bf16[64,1024]{1,0:T(8,128)(2,1)S(1)}, bf16[64,1024]{1,0:T(8,128)(2,1)S(1)}, u32[]{:S(2)}, u32[]{:S(2)}) collective-permute-start(bf16[64,1024]{1,0:T(8,128)(2,1)S(1)} %convert_element_type.35), channel_id=1, source_target_pairs={{0,9},{1,24},{3,10},{2,27},{4,13},{5,28},{7,14},{6,31},{9,0},{8,17... | collective-permute-start | bytes 393224 | tf_op jit(solution)/shard_map/ppermute | solution.py:31
  72.4 0.1 copy.9
  72.5 4.2 %collective-permute-start.3 = (bf16[128,384]{0,1:T(8,128)(2,1)S(1)}, bf16[128,384]{0,1:T(8,128)(2,1)S(1)}, u32[]{:S(2)}, u32[]{:S(2)}) collective-permute-start(bf16[128,384]{0,1:T(8,128)(2,1)S(1)} %get-tuple-element.42), channel_id=1, source_target_pairs={{0,1},{1,0},{2,3},{3,2},{4,5},{5,4},{6,7},{7,6},{8,9},{9,8},{10,11... | collective-permute-start | bytes 294920 | tf_op jit(solution)/shard_map/ppermute | solution.py:21
  76.7 0.0 copy-start
  76.7 2.1 %collective-permute-start.4 = (bf16[128,384]{0,1:T(8,128)(2,1)S(1)}, bf16[128,384]{0,1:T(8,128)(2,1)S(1)}, u32[]{:S(2)}, u32[]{:S(2)}) collective-permute-start(bf16[128,384]{0,1:T(8,128)(2,1)S(1)} %get-tuple-element.41), channel_id=1, source_target_pairs={{0,1},{1,0},{2,3},{3,2},{4,5},{5,4},{6,7},{7,6},{8,9},{9,8},{10,11... | collective-permute-start | bytes 294920 | tf_op jit(solution)/shard_map/ppermute | solution.py:21
  78.8 0.0 collective-permute-done.3
  78.8 1.3 collective-permute-done.4
  80.0 4.3 %collective-permute-done.2 = bf16[64,1024]{1,0:T(8,128)(2,1)S(1)} collective-permute-done((bf16[64,1024]{1,0:T(8,128)(2,1)S(1)}, bf16[64,1024]{1,0:T(8,128)(2,1)S(1)}, u32[]{:S(2)}, u32[]{:S(2)}) %collective-permute-start.2) | collective-permute-done | bytes 131104 | tf_op jit(solution)/shard_map/ppermute | solution.py:31
  84.4 1.9 %collective-permute-start.5 = (bf16[64,1024]{1,0:T(8,128)(2,1)S(1)}, bf16[64,1024]{1,0:T(8,128)(2,1)S(1)}, u32[]{:S(2)}, u32[]{:S(2)}) collective-permute-start(bf16[64,1024]{1,0:T(8,128)(2,1)S(1)} %fusion), channel_id=1, source_target_pairs={{0,25},{1,8},{3,26},{2,11},{4,29},{5,12},{7,30},{6,15},{9,16},{8,1... | collective-permute-start | bytes 393224 | tf_op jit(solution)/shard_map/ppermute | solution.py:31
  86.3 9.5 %collective-permute-done.5 = bf16[64,1024]{1,0:T(8,128)(2,1)S(1)} collective-permute-done((bf16[64,1024]{1,0:T(8,128)(2,1)S(1)}, bf16[64,1024]{1,0:T(8,128)(2,1)S(1)}, u32[]{:S(2)}, u32[]{:S(2)}) %collective-permute-start.5) | collective-permute-done | bytes 131104 | tf_op jit(solution)/shard_map/ppermute | solution.py:31
  95.9 0.1 multiply_convert_fusion
  95.9 2.7 %collective-permute-start.6 = (bf16[64,1024]{1,0:T(8,128)(2,1)S(1)}, bf16[64,1024]{1,0:T(8,128)(2,1)S(1)}, u32[]{:S(2)}, u32[]{:S(2)}) collective-permute-start(bf16[64,1024]{1,0:T(8,128)(2,1)S(1)} %get-tuple-element.39.own_ref), channel_id=1, source_target_pairs={{32,0},{64,32},{96,64},{128,96},{160,128},{192,160},{224,192},{256... | collective-permute-start | bytes 393224 | tf_op jit(solution)/shard_map/ppermute | solution.py:37
  98.6 0.6 fusion.2
  99.3 5.6 %collective-permute-done.6.next_ref = bf16[64,1024]{1,0:T(8,128)(2,1)S(1)} collective-permute-done((bf16[64,1024]{1,0:T(8,128)(2,1)S(1)}, bf16[64,1024]{1,0:T(8,128)(2,1)S(1)}, u32[]{:S(2)}, u32[]{:S(2)}) %collective-permute-start.6) | collective-permute-done | bytes 131104 | tf_op jit(solution)/shard_map/ppermute | solution.py:37
  104.9 0.1 shard_map.78
  105.0 16.0 %all_to_all.11.err_ref = bf16[4,2,64,1024]{3,2,1,0:T(8,128)(2,1)} all-to-all(bf16[4,2,64,1024]{3,2,1,0:T(8,128)(2,1)S(1)} %shard_map.78), channel_id=1, replica_groups={{0,3,4,7},{1,2,5,6},{9,10,13,14},{8,11,12,15},{16,19,20,23},{17,18,21,2..., dimensions={0} | all-to-all | bytes 2097152 | tf_op jit(solution)/shard_map/all_to_all | solution.py:224
  120.9 1.9 %collective-permute-start.7 = (bf16[4,2,64,1024]{3,2,1,0:T(8,128)(2,1)}, bf16[4,2,64,1024]{3,2,1,0:T(8,128)(2,1)S(1)}, u32[]{:S(2)}, u32[]{:S(2)}) collective-permute-start(bf16[4,2,64,1024]{3,2,1,0:T(8,128)(2,1)} %all_to_all.11.err_ref), channel_id=1, source_target_pairs={{0,1},{1,0},{2,3},{3,2},{4,5},{5,4},{6,7},{7,6},{8,9},{9,8},{10,11... | collective-permute-start | bytes 3145736 | tf_op jit(solution)/shard_map/ppermute | solution.py:21
  122.9 0.0 copy-done
  122.9 2.3 %shard_map.79 = (f32[2,384,1024]{2,1,0:T(8,128)S(1)}, bf16[256,384]{1,0:T(8,128)(2,1)S(1)}) custom-call(bf16[4,2,64,1024]{3,2,1,0:T(8,128)(2,1)} %all_to_all.11.err_ref, bf16[384,256]{1,0:T(8,128)(2,1)S(1)} %bitcast.17, bf16[2,384,1024]{2,1,0:T(8,128)(2,1)S(1)} %bitcast.15), custom_call_target="tpu_custom_call" | custom-call | flops 805306368 | bytes 2000000 | tf_op jit(solution)/shard_map/pallas_call | solution.py:147
  125.2 0.5 collective-permute-done.7.err_ref
  125.7 2.0 %shard_map.80 = (bf16[2,384,1024]{2,1,0:T(8,128)(2,1)}, bf16[512,384]{1,0:T(8,128)(2,1)}) custom-call(s32[1]{0:T(128)} %bitcast.8.set_ref, bf16[4,2,64,1024]{3,2,1,0:T(8,128)(2,1)S(1)} %collective-permute-done.7.err_ref, bf16[384,256]{1,0:T(8,128)(2,1)S(1)} %maximum_bitcast_fusion.lat_ref, bf16[2,384,1024]{2,1,0:T(8,128)(2,1)S(1)} %bitcast.16, ...), custom_call_target="tpu_custom_call" | custom-call | flops 805306368 | bytes 2000000 | tf_op jit(solution)/shard_map/pallas_call | solution.py:187
  (7 shorter events, 0.1 us)
Async XLA Ops:
  0.6 3.6 %copy-start.2 = (bf16[1,16,1024]{2,1,0:T(8,128)(2,1)S(1)}, bf16[1,16,1024]{2,1,0:T(8,128)(2,1)}, u32[]{:S(2)}) copy-start(bf16[1,16,1024]{2,1,0:T(8,128)(2,1)} %param.5) | copy-start | bytes 98308
  2.3 26.7 %collective-permute-start = (bf16[1296,1024]{1,0:T(8,128)(2,1)S(1)}, bf16[1296,1024]{1,0:T(8,128)(2,1)S(1)}, u32[]{:S(2)}, u32[]{:S(2)}) collective-permute-start(bf16[1296,1024]{1,0:T(8,128)(2,1)S(1)} %shard_map.76.own_ref), channel_id=1, source_target_pairs={{0,1},{1,0},{2,3},{3,2},{4,5},{5,4},{6,7},{7,6},{8,9},{9,8},{10,11... | collective-permute-start | bytes 7962632 | tf_op jit(solution)/shard_map/ppermute | solution.py:21
  43.8 26.3 %copy-start.1 = (bf16[1,16,1024]{2,1,0:T(8,128)(2,1)S(1)}, bf16[1,16,1024]{2,1,0:T(8,128)(2,1)}, u32[]{:S(2)}) copy-start(bf16[1,16,1024]{2,1,0:T(8,128)(2,1)} %param.6) | copy-start | bytes 98308
  63.2 6.9 %collective-permute-start.1 = (bf16[64,1024]{1,0:T(8,128)(2,1)S(1)}, bf16[64,1024]{1,0:T(8,128)(2,1)S(1)}, u32[]{:S(2)}, u32[]{:S(2)}) collective-permute-start(bf16[64,1024]{1,0:T(8,128)(2,1)S(1)} %slice.23), channel_id=1, source_target_pairs={{0,32},{32,64},{64,96},{96,128},{128,160},{160,192},{192,224},{224... | collective-permute-start | bytes 393224 | tf_op jit(solution)/shard_map/ppermute | solution.py:37
  70.2 14.1 %collective-permute-start.2 = (bf16[64,1024]{1,0:T(8,128)(2,1)S(1)}, bf16[64,1024]{1,0:T(8,128)(2,1)S(1)}, u32[]{:S(2)}, u32[]{:S(2)}) collective-permute-start(bf16[64,1024]{1,0:T(8,128)(2,1)S(1)} %convert_element_type.35), channel_id=1, source_target_pairs={{0,9},{1,24},{3,10},{2,27},{4,13},{5,28},{7,14},{6,31},{9,0},{8,17... | collective-permute-start | bytes 393224 | tf_op jit(solution)/shard_map/ppermute | solution.py:31
  72.5 6.2 %collective-permute-start.3 = (bf16[128,384]{0,1:T(8,128)(2,1)S(1)}, bf16[128,384]{0,1:T(8,128)(2,1)S(1)}, u32[]{:S(2)}, u32[]{:S(2)}) collective-permute-start(bf16[128,384]{0,1:T(8,128)(2,1)S(1)} %get-tuple-element.42), channel_id=1, source_target_pairs={{0,1},{1,0},{2,3},{3,2},{4,5},{5,4},{6,7},{7,6},{8,9},{9,8},{10,11... | collective-permute-start | bytes 294920 | tf_op jit(solution)/shard_map/ppermute | solution.py:21
  76.7 46.2 %copy-start = (bf16[1,2,384,1024]{3,2,1,0:T(8,128)(2,1)S(1)}, bf16[1,2,384,1024]{3,2,1,0:T(8,128)(2,1)}, u32[]{:S(2)}) copy-start(bf16[1,2,384,1024]{3,2,1,0:T(8,128)(2,1)} %param.9) | copy-start | bytes 4718596
  76.7 3.3 %collective-permute-start.4 = (bf16[128,384]{0,1:T(8,128)(2,1)S(1)}, bf16[128,384]{0,1:T(8,128)(2,1)S(1)}, u32[]{:S(2)}, u32[]{:S(2)}) collective-permute-start(bf16[128,384]{0,1:T(8,128)(2,1)S(1)} %get-tuple-element.41), channel_id=1, source_target_pairs={{0,1},{1,0},{2,3},{3,2},{4,5},{5,4},{6,7},{7,6},{8,9},{9,8},{10,11... | collective-permute-start | bytes 294920 | tf_op jit(solution)/shard_map/ppermute | solution.py:21
  84.4 11.5 %collective-permute-start.5 = (bf16[64,1024]{1,0:T(8,128)(2,1)S(1)}, bf16[64,1024]{1,0:T(8,128)(2,1)S(1)}, u32[]{:S(2)}, u32[]{:S(2)}) collective-permute-start(bf16[64,1024]{1,0:T(8,128)(2,1)S(1)} %fusion), channel_id=1, source_target_pairs={{0,25},{1,8},{3,26},{2,11},{4,29},{5,12},{7,30},{6,15},{9,16},{8,1... | collective-permute-start | bytes 393224 | tf_op jit(solution)/shard_map/ppermute | solution.py:31
  95.9 9.0 %collective-permute-start.6 = (bf16[64,1024]{1,0:T(8,128)(2,1)S(1)}, bf16[64,1024]{1,0:T(8,128)(2,1)S(1)}, u32[]{:S(2)}, u32[]{:S(2)}) collective-permute-start(bf16[64,1024]{1,0:T(8,128)(2,1)S(1)} %get-tuple-element.39.own_ref), channel_id=1, source_target_pairs={{32,0},{64,32},{96,64},{128,96},{160,128},{192,160},{224,192},{256... | collective-permute-start | bytes 393224 | tf_op jit(solution)/shard_map/ppermute | solution.py:37
  120.9 4.8 %collective-permute-start.7 = (bf16[4,2,64,1024]{3,2,1,0:T(8,128)(2,1)}, bf16[4,2,64,1024]{3,2,1,0:T(8,128)(2,1)S(1)}, u32[]{:S(2)}, u32[]{:S(2)}) collective-permute-start(bf16[4,2,64,1024]{3,2,1,0:T(8,128)(2,1)} %all_to_all.11.err_ref), channel_id=1, source_target_pairs={{0,1},{1,0},{2,3},{3,2},{4,5},{5,4},{6,7},{7,6},{8,9},{9,8},{10,11... | collective-permute-start | bytes 3145736 | tf_op jit(solution)/shard_map/ppermute | solution.py:21

commit v6 on v5

--- a/solution.py
+++ b/solution.py
@@ -211,11 +211,12 @@
     part = part[:, :1024] + shifted.astype(F32)
     own = lax.dynamic_slice(part, (z_at, 0), (16, 1024)) - target
     part = lax.dynamic_update_slice(part, own, (z_at, 0))
-    halves = [swap_cores(lat_sibling[:128]), swap_cores(lat_sibling[128:])]
-    met, *halves = lax.optimization_barrier((exchange_z(part.astype(BF), 1, 3), *halves))
-    other_t = jnp.concatenate(halves).T
+    met, early = lax.optimization_barrier((exchange_z(part.astype(BF), 1, 3), swap_cores(lat_sibling[:128])))
     part = part + met.astype(F32)
-    part = part + exchange_z(part.astype(BF), 3, 1).astype(F32)
+    part, late = lax.optimization_barrier((part, lat_sibling[128:]))
+    met, late = lax.optimization_barrier((exchange_z(part.astype(BF), 3, 1), swap_cores(late)))
+    part = part + met.astype(F32)
+    other_t = jnp.concatenate([early, late]).T
     recon = (lax.dynamic_slice(part, (z_at, 0), (16, 1024)) + target).astype(BF)
 
     error = (0.25 * part).astype(BF)

time: 129 us -> 129 us (level)
  starting transfers between devices: 19.7 us -> 22.4 us
  waiting for transfers between devices: 25 us -> 22.5 us
    ppermute x2, waiting for transfers between devices: 13.8 us -> 10.7 us  [exchange_z(): return lax.ppermute(block, 'latent', route)]
    ppermute x4, starting transfers between devices: 10 us -> 12.6 us  [swap_cores(): return lax.ppermute(block, 'latent', [(i, i ^ 1) for i in range(32)])]
  transfers between devices with their start and end apart: 8 -> 8, of which waited for: 6 -> 7; matrix products, arithmetic and copies ran while one was open for 1% -> 1% of each run, Pallas kernels for 2% -> 2%
where the time goes in v6:
time: 129 us; the launch traced here: 128 us
  blocking collectives  72.9 us (57%)
  waiting for transfers between devices  22.5 us (17%)
  starting transfers between devices  22.4 us (17%)
  Pallas kernels  7.93 us (6%)
    all_gather x1, blocking collectives, per_device(): lax.all_gather(residual[0], 'latent', axis=0, tiled=True, axis_index_grou...  24.7 us
    all_to_all x1, blocking collectives, per_device(): lax.all_to_all(part, 'latent', 0, 0, tiled=True, axis_index_groups=ALONG_Y)  19.2 us
    all_to_all x1, blocking collectives, per_device(): lax.all_to_all(both, 'latent', 0, 0, tiled=True, axis_index_groups=ALONG_Y)  16 us
    all_gather x1, blocking collectives, per_device(): lax.all_gather(mine, 'latent', axis=0, tiled=True, axis_index_groups=ALON...  12.9 us
    ppermute x4, starting transfers between devices, swap_cores(): return lax.ppermute(block, 'latent', [(i, i ^ 1) for i in range(32)])  12.6 us
    ppermute x2, waiting for transfers between devices, exchange_z(): return lax.ppermute(block, 'latent', route)  10.7 us
    ppermute x2, waiting for transfers between devices, shift_layer(): return lax.ppermute(block, 'layer', route)  9.42 us
    ppermute x2, starting transfers between devices, shift_layer(): return lax.ppermute(block, 'layer', route)  5.56 us
  transfers between devices with their start and end apart: 8, of which 7 were waited for; matrix products, arithmetic and copies ran while one was open for 1% of the time, Pallas kernels for 2%

profile of v6, /device:TPU:6, one launch (start us, length us, event | category | flops | bytes accessed | tf_op | source)
XLA Modules:
  0.0 127.8 jit_solution(2911888709882172282)
XLA Ops:
  0.6 0.0 copy-start.2
  0.6 1.7 %shard_map.76.own_ref = bf16[1296,1024]{1,0:T(8,128)(2,1)S(1)} custom-call(bf16[1024,384]{1,0:T(8,128)(2,1)} %bitcast.18, f32[1,384]{1,0:T(1,128)} %bias_ref.1, bf16[2,384,1024]{2,1,0:T(8,128)(2,1)} %bitcast.14), custom_call_target="tpu_custom_call" | custom-call | flops 1 | bytes 2000000 | tf_op jit(solution)/shard_map/pallas_call | solution.py:86
  2.3 1.9 %collective-permute-start = (bf16[1296,1024]{1,0:T(8,128)(2,1)S(1)}, bf16[1296,1024]{1,0:T(8,128)(2,1)S(1)}, u32[]{:S(2)}, u32[]{:S(2)}) collective-permute-start(bf16[1296,1024]{1,0:T(8,128)(2,1)S(1)} %shard_map.76.own_ref), channel_id=1, source_target_pairs={{0,1},{1,0},{2,3},{3,2},{4,5},{5,4},{6,7},{7,6},{8,9},{9,8},{10,11... | collective-permute-start | bytes 7962632 | tf_op jit(solution)/shard_map/ppermute | solution.py:21
  4.3 0.0 copy-done.2
  4.3 24.7 %all-gather = bf16[1,64,1024]{2,1,0:T(8,128)(2,1)S(1)} all-gather(bf16[1,16,1024]{2,1,0:T(8,128)(2,1)S(1)} %copy-done.2), channel_id=2, replica_groups={{0,9,16,25},{1,8,17,24},{3,10,19,26},{2,11,18,27},{4,13,20,29},{5,12,21..., dimensions={1}, use_global_device_ids=true | all-gather | bytes 163840 | tf_op jit(solution)/shard_map/all_gather | solution.py:203
  29.0 0.0 collective-permute-done.sib_ref
  29.0 12.9 %all_gather.7.rows_ref = bf16[256,1024]{1,0:T(8,128)(2,1)S(1)} all-gather(bf16[64,1024]{1,0:T(8,128)(2,1)S(1)} %bitcast.19), channel_id=1, replica_groups={{0,3,4,7},{1,2,5,6},{9,10,13,14},{8,11,12,15},{16,19,20,23},{17,18,21,2..., dimensions={0}, use_global_device_ids=true | all-gather | bytes 655360 | tf_op jit(solution)/shard_map/all_gather | solution.py:205
  42.0 1.9 %shard_map.77 = (bf16[4,64,2048]{2,1,0:T(8,128)(2,1)S(1)}, bf16[256,384]{1,0:T(8,128)(2,1)S(1)}, bf16[256,384]{1,0:T(8,128)(2,1)S(1)}) custom-call(bf16[256,1024]{1,0:T(8,128)(2,1)S(1)} %all_gather.7.rows_ref, bf16[1296,1024]{1,0:T(8,128)(2,1)S(1)} %shard_map.76.own_ref, bf16[1296,1024]{1,0:T(8,128)(2,1)S(1)} %collective-permute-done.sib_ref), custom_call_target="tpu_custom_call" | custom-call | flops 1207959552 | bytes 2000000 | tf_op jit(solution)/shard_map/pallas_call | solution.py:115
  43.8 0.0 copy-start.1
  43.8 19.2 %all_to_all.10 = bf16[4,64,2048]{2,1,0:T(8,128)(2,1)S(1)} all-to-all(bf16[4,64,2048]{2,1,0:T(8,128)(2,1)S(1)} %get-tuple-element.26), channel_id=1, replica_groups={{0,3,4,7},{1,2,5,6},{9,10,13,14},{8,11,12,15},{16,19,20,23},{17,18,21,2..., dimensions={0} | all-to-all | bytes 2097152 | tf_op jit(solution)/shard_map/all_to_all | solution.py:207
  63.1 0.2 convert_reduce_fusion
  63.2 2.8 %collective-permute-start.1 = (bf16[64,1024]{1,0:T(8,128)(2,1)S(1)}, bf16[64,1024]{1,0:T(8,128)(2,1)S(1)}, u32[]{:S(2)}, u32[]{:S(2)}) collective-permute-start(bf16[64,1024]{1,0:T(8,128)(2,1)S(1)} %slice.23), channel_id=1, source_target_pairs={{0,32},{32,64},{64,96},{96,128},{128,160},{160,192},{192,224},{224... | collective-permute-start | bytes 393224 | tf_op jit(solution)/shard_map/ppermute | solution.py:37
  66.1 0.1 copy.8
  66.3 3.8 %collective-permute-done.1 = bf16[64,1024]{1,0:T(8,128)(2,1)S(1)} collective-permute-done((bf16[64,1024]{1,0:T(8,128)(2,1)S(1)}, bf16[64,1024]{1,0:T(8,128)(2,1)S(1)}, u32[]{:S(2)}, u32[]{:S(2)}) %collective-permute-start.1) | collective-permute-done | bytes 131104 | tf_op jit(solution)/shard_map/ppermute | solution.py:37
  70.1 0.0 copy-done.1
  70.2 2.2 %collective-permute-start.2 = (bf16[64,1024]{1,0:T(8,128)(2,1)S(1)}, bf16[64,1024]{1,0:T(8,128)(2,1)S(1)}, u32[]{:S(2)}, u32[]{:S(2)}) collective-permute-start(bf16[64,1024]{1,0:T(8,128)(2,1)S(1)} %convert_element_type.35), channel_id=1, source_target_pairs={{0,9},{1,24},{3,10},{2,27},{4,13},{5,28},{7,14},{6,31},{9,0},{8,17... | collective-permute-start | bytes 393224 | tf_op jit(solution)/shard_map/ppermute | solution.py:31
  72.4 0.1 copy.9
  72.5 4.2 %collective-permute-start.3 = (bf16[128,384]{0,1:T(8,128)(2,1)S(1)}, bf16[128,384]{0,1:T(8,128)(2,1)S(1)}, u32[]{:S(2)}, u32[]{:S(2)}) collective-permute-start(bf16[128,384]{0,1:T(8,128)(2,1)S(1)} %get-tuple-element.48), channel_id=1, source_target_pairs={{0,1},{1,0},{2,3},{3,2},{4,5},{5,4},{6,7},{7,6},{8,9},{9,8},{10,11... | collective-permute-start | bytes 294920 | tf_op jit(solution)/shard_map/ppermute | solution.py:21
  76.7 0.9 collective-permute-done.3
  77.6 6.7 %collective-permute-done.2 = bf16[64,1024]{1,0:T(8,128)(2,1)S(1)} collective-permute-done((bf16[64,1024]{1,0:T(8,128)(2,1)S(1)}, bf16[64,1024]{1,0:T(8,128)(2,1)S(1)}, u32[]{:S(2)}, u32[]{:S(2)}) %collective-permute-start.2) | collective-permute-done | bytes 131104 | tf_op jit(solution)/shard_map/ppermute | solution.py:31
  84.4 0.0 copy-start
  84.4 2.1 %collective-permute-start.4 = (bf16[64,1024]{1,0:T(8,128)(2,1)S(1)}, bf16[64,1024]{1,0:T(8,128)(2,1)S(1)}, u32[]{:S(2)}, u32[]{:S(2)}) collective-permute-start(bf16[64,1024]{1,0:T(8,128)(2,1)S(1)} %convert_element_type.37), channel_id=1, source_target_pairs={{0,25},{1,8},{3,26},{2,11},{4,29},{5,12},{7,30},{6,15},{9,16},{8,1... | collective-permute-start | bytes 393224 | tf_op jit(solution)/shard_map/ppermute | solution.py:31
  86.5 4.6 %collective-permute-start.5 = (bf16[128,384]{0,1:T(8,128)(2,1)S(1)}, bf16[128,384]{0,1:T(8,128)(2,1)S(1)}, u32[]{:S(2)}, u32[]{:S(2)}) collective-permute-start(bf16[128,384]{0,1:T(8,128)(2,1)S(1)} %get-tuple-element.33), channel_id=1, source_target_pairs={{0,1},{1,0},{2,3},{3,2},{4,5},{5,4},{6,7},{7,6},{8,9},{9,8},{10,11... | collective-permute-start | bytes 294920 | tf_op jit(solution)/shard_map/ppermute | solution.py:21
  91.1 0.9 collective-permute-done.5
  92.0 4.0 %collective-permute-done.4 = bf16[64,1024]{1,0:T(8,128)(2,1)S(1)} collective-permute-done((bf16[64,1024]{1,0:T(8,128)(2,1)S(1)}, bf16[64,1024]{1,0:T(8,128)(2,1)S(1)}, u32[]{:S(2)}, u32[]{:S(2)}) %collective-permute-start.4) | collective-permute-done | bytes 131104 | tf_op jit(solution)/shard_map/ppermute | solution.py:31
  96.1 2.7 %collective-permute-start.6 = (bf16[64,1024]{1,0:T(8,128)(2,1)S(1)}, bf16[64,1024]{1,0:T(8,128)(2,1)S(1)}, u32[]{:S(2)}, u32[]{:S(2)}) collective-permute-start(bf16[64,1024]{1,0:T(8,128)(2,1)S(1)} %get-tuple-element.45.own_ref), channel_id=1, source_target_pairs={{32,0},{64,32},{96,64},{128,96},{160,128},{192,160},{224,192},{256... | collective-permute-start | bytes 393224 | tf_op jit(solution)/shard_map/ppermute | solution.py:37
  98.8 0.6 fusion.1
  99.5 5.6 %collective-permute-done.6.next_ref = bf16[64,1024]{1,0:T(8,128)(2,1)S(1)} collective-permute-done((bf16[64,1024]{1,0:T(8,128)(2,1)S(1)}, bf16[64,1024]{1,0:T(8,128)(2,1)S(1)}, u32[]{:S(2)}, u32[]{:S(2)}) %collective-permute-start.6) | collective-permute-done | bytes 131104 | tf_op jit(solution)/shard_map/ppermute | solution.py:37
  105.0 0.1 shard_map.78
  105.1 16.0 %all_to_all.11.err_ref = bf16[4,2,64,1024]{3,2,1,0:T(8,128)(2,1)} all-to-all(bf16[4,2,64,1024]{3,2,1,0:T(8,128)(2,1)S(1)} %shard_map.78), channel_id=1, replica_groups={{0,3,4,7},{1,2,5,6},{9,10,13,14},{8,11,12,15},{16,19,20,23},{17,18,21,2..., dimensions={0} | all-to-all | bytes 2097152 | tf_op jit(solution)/shard_map/all_to_all | solution.py:225
  121.1 1.9 %collective-permute-start.7 = (bf16[4,2,64,1024]{3,2,1,0:T(8,128)(2,1)}, bf16[4,2,64,1024]{3,2,1,0:T(8,128)(2,1)S(1)}, u32[]{:S(2)}, u32[]{:S(2)}) collective-permute-start(bf16[4,2,64,1024]{3,2,1,0:T(8,128)(2,1)} %all_to_all.11.err_ref), channel_id=1, source_target_pairs={{0,1},{1,0},{2,3},{3,2},{4,5},{5,4},{6,7},{7,6},{8,9},{9,8},{10,11... | collective-permute-start | bytes 3145736 | tf_op jit(solution)/shard_map/ppermute | solution.py:21
  123.0 0.0 copy-done
  123.0 2.3 %shard_map.79 = (f32[2,384,1024]{2,1,0:T(8,128)S(1)}, bf16[256,384]{1,0:T(8,128)(2,1)S(1)}) custom-call(bf16[4,2,64,1024]{3,2,1,0:T(8,128)(2,1)} %all_to_all.11.err_ref, bf16[384,256]{1,0:T(8,128)(2,1)S(1)} %bitcast.17, bf16[2,384,1024]{2,1,0:T(8,128)(2,1)S(1)} %bitcast.15), custom_call_target="tpu_custom_call" | custom-call | flops 805306368 | bytes 2000000 | tf_op jit(solution)/shard_map/pallas_call | solution.py:147
  125.4 0.5 collective-permute-done.7.err_ref
  125.8 2.0 %shard_map.80 = (bf16[2,384,1024]{2,1,0:T(8,128)(2,1)}, bf16[512,384]{1,0:T(8,128)(2,1)}) custom-call(s32[1]{0:T(128)} %bitcast.8.set_ref, bf16[4,2,64,1024]{3,2,1,0:T(8,128)(2,1)S(1)} %collective-permute-done.7.err_ref, bf16[384,256]{1,0:T(8,128)(2,1)S(1)} %maximum_bitcast_fusion.lat_ref, bf16[2,384,1024]{2,1,0:T(8,128)(2,1)S(1)} %bitcast.16, ...), custom_call_target="tpu_custom_call" | custom-call | flops 805306368 | bytes 2000000 | tf_op jit(solution)/shard_map/pallas_call | solution.py:187
  (9 shorter events, 0.2 us)
Async XLA Ops:
  0.6 3.6 %copy-start.2 = (bf16[1,16,1024]{2,1,0:T(8,128)(2,1)S(1)}, bf16[1,16,1024]{2,1,0:T(8,128)(2,1)}, u32[]{:S(2)}) copy-start(bf16[1,16,1024]{2,1,0:T(8,128)(2,1)} %param.5) | copy-start | bytes 98308
  2.3 26.7 %collective-permute-start = (bf16[1296,1024]{1,0:T(8,128)(2,1)S(1)}, bf16[1296,1024]{1,0:T(8,128)(2,1)S(1)}, u32[]{:S(2)}, u32[]{:S(2)}) collective-permute-start(bf16[1296,1024]{1,0:T(8,128)(2,1)S(1)} %shard_map.76.own_ref), channel_id=1, source_target_pairs={{0,1},{1,0},{2,3},{3,2},{4,5},{5,4},{6,7},{7,6},{8,9},{9,8},{10,11... | collective-permute-start | bytes 7962632 | tf_op jit(solution)/shard_map/ppermute | solution.py:21
  43.8 26.3 %copy-start.1 = (bf16[1,16,1024]{2,1,0:T(8,128)(2,1)S(1)}, bf16[1,16,1024]{2,1,0:T(8,128)(2,1)}, u32[]{:S(2)}) copy-start(bf16[1,16,1024]{2,1,0:T(8,128)(2,1)} %param.6) | copy-start | bytes 98308
  63.2 6.9 %collective-permute-start.1 = (bf16[64,1024]{1,0:T(8,128)(2,1)S(1)}, bf16[64,1024]{1,0:T(8,128)(2,1)S(1)}, u32[]{:S(2)}, u32[]{:S(2)}) collective-permute-start(bf16[64,1024]{1,0:T(8,128)(2,1)S(1)} %slice.23), channel_id=1, source_target_pairs={{0,32},{32,64},{64,96},{96,128},{128,160},{160,192},{192,224},{224... | collective-permute-start | bytes 393224 | tf_op jit(solution)/shard_map/ppermute | solution.py:37
  70.2 14.1 %collective-permute-start.2 = (bf16[64,1024]{1,0:T(8,128)(2,1)S(1)}, bf16[64,1024]{1,0:T(8,128)(2,1)S(1)}, u32[]{:S(2)}, u32[]{:S(2)}) collective-permute-start(bf16[64,1024]{1,0:T(8,128)(2,1)S(1)} %convert_element_type.35), channel_id=1, source_target_pairs={{0,9},{1,24},{3,10},{2,27},{4,13},{5,28},{7,14},{6,31},{9,0},{8,17... | collective-permute-start | bytes 393224 | tf_op jit(solution)/shard_map/ppermute | solution.py:31
  72.5 5.1 %collective-permute-start.3 = (bf16[128,384]{0,1:T(8,128)(2,1)S(1)}, bf16[128,384]{0,1:T(8,128)(2,1)S(1)}, u32[]{:S(2)}, u32[]{:S(2)}) collective-permute-start(bf16[128,384]{0,1:T(8,128)(2,1)S(1)} %get-tuple-element.48), channel_id=1, source_target_pairs={{0,1},{1,0},{2,3},{3,2},{4,5},{5,4},{6,7},{7,6},{8,9},{9,8},{10,11... | collective-permute-start | bytes 294920 | tf_op jit(solution)/shard_map/ppermute | solution.py:21
  84.4 38.6 %copy-start = (bf16[1,2,384,1024]{3,2,1,0:T(8,128)(2,1)S(1)}, bf16[1,2,384,1024]{3,2,1,0:T(8,128)(2,1)}, u32[]{:S(2)}) copy-start(bf16[1,2,384,1024]{3,2,1,0:T(8,128)(2,1)} %param.9) | copy-start | bytes 4718596
  84.4 11.6 %collective-permute-start.4 = (bf16[64,1024]{1,0:T(8,128)(2,1)S(1)}, bf16[64,1024]{1,0:T(8,128)(2,1)S(1)}, u32[]{:S(2)}, u32[]{:S(2)}) collective-permute-start(bf16[64,1024]{1,0:T(8,128)(2,1)S(1)} %convert_element_type.37), channel_id=1, source_target_pairs={{0,25},{1,8},{3,26},{2,11},{4,29},{5,12},{7,30},{6,15},{9,16},{8,1... | collective-permute-start | bytes 393224 | tf_op jit(solution)/shard_map/ppermute | solution.py:31
  86.5 5.6 %collective-permute-start.5 = (bf16[128,384]{0,1:T(8,128)(2,1)S(1)}, bf16[128,384]{0,1:T(8,128)(2,1)S(1)}, u32[]{:S(2)}, u32[]{:S(2)}) collective-permute-start(bf16[128,384]{0,1:T(8,128)(2,1)S(1)} %get-tuple-element.33), channel_id=1, source_target_pairs={{0,1},{1,0},{2,3},{3,2},{4,5},{5,4},{6,7},{7,6},{8,9},{9,8},{10,11... | collective-permute-start | bytes 294920 | tf_op jit(solution)/shard_map/ppermute | solution.py:21
  96.1 9.0 %collective-permute-start.6 = (bf16[64,1024]{1,0:T(8,128)(2,1)S(1)}, bf16[64,1024]{1,0:T(8,128)(2,1)S(1)}, u32[]{:S(2)}, u32[]{:S(2)}) collective-permute-start(bf16[64,1024]{1,0:T(8,128)(2,1)S(1)} %get-tuple-element.45.own_ref), channel_id=1, source_target_pairs={{32,0},{64,32},{96,64},{128,96},{160,128},{192,160},{224,192},{256... | collective-permute-start | bytes 393224 | tf_op jit(solution)/shard_map/ppermute | solution.py:37
  121.1 4.8 %collective-permute-start.7 = (bf16[4,2,64,1024]{3,2,1,0:T(8,128)(2,1)}, bf16[4,2,64,1024]{3,2,1,0:T(8,128)(2,1)S(1)}, u32[]{:S(2)}, u32[]{:S(2)}) collective-permute-start(bf16[4,2,64,1024]{3,2,1,0:T(8,128)(2,1)} %all_to_all.11.err_ref), channel_id=1, source_target_pairs={{0,1},{1,0},{2,3},{3,2},{4,5},{5,4},{6,7},{7,6},{8,9},{9,8},{10,11... | collective-permute-start | bytes 3145736 | tf_op jit(solution)/shard_map/ppermute | solution.py:21

commit v7 on v5

--- a/solution.py
+++ b/solution.py
@@ -160,11 +160,6 @@
         pltpu.make_async_copy(lat_buf.at[pl.ds(256 * i, 256)], lat_out.at[pl.ds(256 * i, 256)], sems.at[6 + i])
         for i in range(2)
     ]
-    for s in range(2):
-        total = parts_ref[s] + jnp.dot(lat_ref[...], rows_of(err_ref, s), preferred_element_type=F32)
-        dec_buf[s] = total.astype(BF)
-        for i in range(3):
-            sends[3 * s + i].start()
     total = latent_rows(err_ref, dec_ref)
     for z in range(4):
         for y in range(4):
@@ -176,6 +171,11 @@
             lat_buf[pl.ds(pl.multiple_of(there + away, 16), 16), :] = total[here : here + 16, :]
         if z % 2:
             sends[6 + z // 2].start()
+    for s in range(2):
+        total = parts_ref[s] + jnp.dot(lat_ref[...], rows_of(err_ref, s), preferred_element_type=F32)
+        dec_buf[s] = total.astype(BF)
+        for i in range(3):
+            sends[3 * s + i].start()
     for send in sends:
         send.wait()
 

time: 129 us -> 129 us (level)
  no operation moved by 1% of the time
where the time goes in v7:
time: 129 us; the launch traced here: 128 us
  blocking collectives  72.9 us (57%)
  waiting for transfers between devices  25 us (19%)
  starting transfers between devices  19.7 us (15%)
  Pallas kernels  8.15 us (6%)
    all_gather x1, blocking collectives, per_device(): lax.all_gather(residual[0], 'latent', axis=0, tiled=True, axis_index_grou...  24.7 us
    all_to_all x1, blocking collectives, per_device(): lax.all_to_all(part, 'latent', 0, 0, tiled=True, axis_index_groups=ALONG_Y)  19.2 us
    all_to_all x1, blocking collectives, per_device(): lax.all_to_all(both, 'latent', 0, 0, tiled=True, axis_index_groups=ALONG_Y)  16 us
    ppermute x2, waiting for transfers between devices, exchange_z(): return lax.ppermute(block, 'latent', route)  13.8 us
    all_gather x1, blocking collectives, per_device(): lax.all_gather(mine, 'latent', axis=0, tiled=True, axis_index_groups=ALON...  12.9 us
    ppermute x4, starting transfers between devices, swap_cores(): return lax.ppermute(block, 'latent', [(i, i ^ 1) for i in range(32)])  10 us
    ppermute x2, waiting for transfers between devices, shift_layer(): return lax.ppermute(block, 'layer', route)  9.45 us
    ppermute x2, starting transfers between devices, shift_layer(): return lax.ppermute(block, 'layer', route)  5.56 us
  transfers between devices with their start and end apart: 8, of which 6 were waited for; matrix products, arithmetic and copies ran while one was open for 1% of the time, Pallas kernels for 2%

profile of v7, /device:TPU:6, one launch (start us, length us, event | category | flops | bytes accessed | tf_op | source)
XLA Modules:
  0.0 127.9 jit_solution(3371866580094192505)
XLA Ops:
  0.6 0.0 copy-start.2
  0.6 1.7 %shard_map.76.own_ref = bf16[1296,1024]{1,0:T(8,128)(2,1)S(1)} custom-call(bf16[1024,384]{1,0:T(8,128)(2,1)} %bitcast.18, f32[1,384]{1,0:T(1,128)} %bias_ref.1, bf16[2,384,1024]{2,1,0:T(8,128)(2,1)} %bitcast.14), custom_call_target="tpu_custom_call" | custom-call | flops 1 | bytes 2000000 | tf_op jit(solution)/shard_map/pallas_call | solution.py:86
  2.3 1.9 %collective-permute-start = (bf16[1296,1024]{1,0:T(8,128)(2,1)S(1)}, bf16[1296,1024]{1,0:T(8,128)(2,1)S(1)}, u32[]{:S(2)}, u32[]{:S(2)}) collective-permute-start(bf16[1296,1024]{1,0:T(8,128)(2,1)S(1)} %shard_map.76.own_ref), channel_id=1, source_target_pairs={{0,1},{1,0},{2,3},{3,2},{4,5},{5,4},{6,7},{7,6},{8,9},{9,8},{10,11... | collective-permute-start | bytes 7962632 | tf_op jit(solution)/shard_map/ppermute | solution.py:21
  4.3 0.0 copy-done.2
  4.3 24.7 %all-gather = bf16[1,64,1024]{2,1,0:T(8,128)(2,1)S(1)} all-gather(bf16[1,16,1024]{2,1,0:T(8,128)(2,1)S(1)} %copy-done.2), channel_id=2, replica_groups={{0,9,16,25},{1,8,17,24},{3,10,19,26},{2,11,18,27},{4,13,20,29},{5,12,21..., dimensions={1}, use_global_device_ids=true | all-gather | bytes 163840 | tf_op jit(solution)/shard_map/all_gather | solution.py:203
  29.0 0.0 collective-permute-done.sib_ref
  29.0 12.9 %all_gather.7.rows_ref = bf16[256,1024]{1,0:T(8,128)(2,1)S(1)} all-gather(bf16[64,1024]{1,0:T(8,128)(2,1)S(1)} %bitcast.19), channel_id=1, replica_groups={{0,3,4,7},{1,2,5,6},{9,10,13,14},{8,11,12,15},{16,19,20,23},{17,18,21,2..., dimensions={0}, use_global_device_ids=true | all-gather | bytes 655360 | tf_op jit(solution)/shard_map/all_gather | solution.py:205
  42.0 1.9 %shard_map.77 = (bf16[4,64,2048]{2,1,0:T(8,128)(2,1)S(1)}, bf16[256,384]{1,0:T(8,128)(2,1)S(1)}, bf16[256,384]{1,0:T(8,128)(2,1)S(1)}) custom-call(bf16[256,1024]{1,0:T(8,128)(2,1)S(1)} %all_gather.7.rows_ref, bf16[1296,1024]{1,0:T(8,128)(2,1)S(1)} %shard_map.76.own_ref, bf16[1296,1024]{1,0:T(8,128)(2,1)S(1)} %collective-permute-done.sib_ref), custom_call_target="tpu_custom_call" | custom-call | flops 1207959552 | bytes 2000000 | tf_op jit(solution)/shard_map/pallas_call | solution.py:115
  43.8 0.0 copy-start.1
  43.8 19.2 %all_to_all.10 = bf16[4,64,2048]{2,1,0:T(8,128)(2,1)S(1)} all-to-all(bf16[4,64,2048]{2,1,0:T(8,128)(2,1)S(1)} %get-tuple-element.23), channel_id=1, replica_groups={{0,3,4,7},{1,2,5,6},{9,10,13,14},{8,11,12,15},{16,19,20,23},{17,18,21,2..., dimensions={0} | all-to-all | bytes 2097152 | tf_op jit(solution)/shard_map/all_to_all | solution.py:207
  63.1 0.2 convert_reduce_fusion
  63.2 2.8 %collective-permute-start.1 = (bf16[64,1024]{1,0:T(8,128)(2,1)S(1)}, bf16[64,1024]{1,0:T(8,128)(2,1)S(1)}, u32[]{:S(2)}, u32[]{:S(2)}) collective-permute-start(bf16[64,1024]{1,0:T(8,128)(2,1)S(1)} %slice.23), channel_id=1, source_target_pairs={{0,32},{32,64},{64,96},{96,128},{128,160},{160,192},{192,224},{224... | collective-permute-start | bytes 393224 | tf_op jit(solution)/shard_map/ppermute | solution.py:37
  66.1 0.1 copy.8
  66.3 3.8 %collective-permute-done.1 = bf16[64,1024]{1,0:T(8,128)(2,1)S(1)} collective-permute-done((bf16[64,1024]{1,0:T(8,128)(2,1)S(1)}, bf16[64,1024]{1,0:T(8,128)(2,1)S(1)}, u32[]{:S(2)}, u32[]{:S(2)}) %collective-permute-start.1) | collective-permute-done | bytes 131104 | tf_op jit(solution)/shard_map/ppermute | solution.py:37
  70.1 0.0 copy-done.1
  70.2 2.2 %collective-permute-start.2 = (bf16[64,1024]{1,0:T(8,128)(2,1)S(1)}, bf16[64,1024]{1,0:T(8,128)(2,1)S(1)}, u32[]{:S(2)}, u32[]{:S(2)}) collective-permute-start(bf16[64,1024]{1,0:T(8,128)(2,1)S(1)} %convert_element_type.35), channel_id=1, source_target_pairs={{0,9},{1,24},{3,10},{2,27},{4,13},{5,28},{7,14},{6,31},{9,0},{8,17... | collective-permute-start | bytes 393224 | tf_op jit(solution)/shard_map/ppermute | solution.py:31
  72.4 0.1 copy.9
  72.5 4.2 %collective-permute-start.3 = (bf16[128,384]{0,1:T(8,128)(2,1)S(1)}, bf16[128,384]{0,1:T(8,128)(2,1)S(1)}, u32[]{:S(2)}, u32[]{:S(2)}) collective-permute-start(bf16[128,384]{0,1:T(8,128)(2,1)S(1)} %get-tuple-element.42), channel_id=1, source_target_pairs={{0,1},{1,0},{2,3},{3,2},{4,5},{5,4},{6,7},{7,6},{8,9},{9,8},{10,11... | collective-permute-start | bytes 294920 | tf_op jit(solution)/shard_map/ppermute | solution.py:21
  76.7 0.0 copy-start
  76.7 2.1 %collective-permute-start.4 = (bf16[128,384]{0,1:T(8,128)(2,1)S(1)}, bf16[128,384]{0,1:T(8,128)(2,1)S(1)}, u32[]{:S(2)}, u32[]{:S(2)}) collective-permute-start(bf16[128,384]{0,1:T(8,128)(2,1)S(1)} %get-tuple-element.41), channel_id=1, source_target_pairs={{0,1},{1,0},{2,3},{3,2},{4,5},{5,4},{6,7},{7,6},{8,9},{9,8},{10,11... | collective-permute-start | bytes 294920 | tf_op jit(solution)/shard_map/ppermute | solution.py:21
  78.8 0.0 collective-permute-done.3
  78.8 1.3 collective-permute-done.4
  80.0 4.3 %collective-permute-done.2 = bf16[64,1024]{1,0:T(8,128)(2,1)S(1)} collective-permute-done((bf16[64,1024]{1,0:T(8,128)(2,1)S(1)}, bf16[64,1024]{1,0:T(8,128)(2,1)S(1)}, u32[]{:S(2)}, u32[]{:S(2)}) %collective-permute-start.2) | collective-permute-done | bytes 131104 | tf_op jit(solution)/shard_map/ppermute | solution.py:31
  84.4 1.9 %collective-permute-start.5 = (bf16[64,1024]{1,0:T(8,128)(2,1)S(1)}, bf16[64,1024]{1,0:T(8,128)(2,1)S(1)}, u32[]{:S(2)}, u32[]{:S(2)}) collective-permute-start(bf16[64,1024]{1,0:T(8,128)(2,1)S(1)} %fusion), channel_id=1, source_target_pairs={{0,25},{1,8},{3,26},{2,11},{4,29},{5,12},{7,30},{6,15},{9,16},{8,1... | collective-permute-start | bytes 393224 | tf_op jit(solution)/shard_map/ppermute | solution.py:31
  86.3 9.5 %collective-permute-done.5 = bf16[64,1024]{1,0:T(8,128)(2,1)S(1)} collective-permute-done((bf16[64,1024]{1,0:T(8,128)(2,1)S(1)}, bf16[64,1024]{1,0:T(8,128)(2,1)S(1)}, u32[]{:S(2)}, u32[]{:S(2)}) %collective-permute-start.5) | collective-permute-done | bytes 131104 | tf_op jit(solution)/shard_map/ppermute | solution.py:31
  95.9 0.1 multiply_convert_fusion
  95.9 2.7 %collective-permute-start.6 = (bf16[64,1024]{1,0:T(8,128)(2,1)S(1)}, bf16[64,1024]{1,0:T(8,128)(2,1)S(1)}, u32[]{:S(2)}, u32[]{:S(2)}) collective-permute-start(bf16[64,1024]{1,0:T(8,128)(2,1)S(1)} %get-tuple-element.39.own_ref), channel_id=1, source_target_pairs={{32,0},{64,32},{96,64},{128,96},{160,128},{192,160},{224,192},{256... | collective-permute-start | bytes 393224 | tf_op jit(solution)/shard_map/ppermute | solution.py:37
  98.6 0.6 fusion.2
  99.3 5.6 %collective-permute-done.6.next_ref = bf16[64,1024]{1,0:T(8,128)(2,1)S(1)} collective-permute-done((bf16[64,1024]{1,0:T(8,128)(2,1)S(1)}, bf16[64,1024]{1,0:T(8,128)(2,1)S(1)}, u32[]{:S(2)}, u32[]{:S(2)}) %collective-permute-start.6) | collective-permute-done | bytes 131104 | tf_op jit(solution)/shard_map/ppermute | solution.py:37
  104.9 0.1 shard_map.78
  105.0 16.0 %all_to_all.11.err_ref = bf16[4,2,64,1024]{3,2,1,0:T(8,128)(2,1)} all-to-all(bf16[4,2,64,1024]{3,2,1,0:T(8,128)(2,1)S(1)} %shard_map.78), channel_id=1, replica_groups={{0,3,4,7},{1,2,5,6},{9,10,13,14},{8,11,12,15},{16,19,20,23},{17,18,21,2..., dimensions={0} | all-to-all | bytes 2097152 | tf_op jit(solution)/shard_map/all_to_all | solution.py:224
  120.9 1.9 %collective-permute-start.7 = (bf16[4,2,64,1024]{3,2,1,0:T(8,128)(2,1)}, bf16[4,2,64,1024]{3,2,1,0:T(8,128)(2,1)S(1)}, u32[]{:S(2)}, u32[]{:S(2)}) collective-permute-start(bf16[4,2,64,1024]{3,2,1,0:T(8,128)(2,1)} %all_to_all.11.err_ref), channel_id=1, source_target_pairs={{0,1},{1,0},{2,3},{3,2},{4,5},{5,4},{6,7},{7,6},{8,9},{9,8},{10,11... | collective-permute-start | bytes 3145736 | tf_op jit(solution)/shard_map/ppermute | solution.py:21
  122.9 0.0 copy-done
  122.9 2.3 %shard_map.79 = (f32[2,384,1024]{2,1,0:T(8,128)S(1)}, bf16[256,384]{1,0:T(8,128)(2,1)S(1)}) custom-call(bf16[4,2,64,1024]{3,2,1,0:T(8,128)(2,1)} %all_to_all.11.err_ref, bf16[384,256]{1,0:T(8,128)(2,1)S(1)} %bitcast.17, bf16[2,384,1024]{2,1,0:T(8,128)(2,1)S(1)} %bitcast.15), custom_call_target="tpu_custom_call" | custom-call | flops 805306368 | bytes 2000000 | tf_op jit(solution)/shard_map/pallas_call | solution.py:147
  125.2 0.5 collective-permute-done.7.err_ref
  125.7 2.2 %shard_map.80 = (bf16[2,384,1024]{2,1,0:T(8,128)(2,1)}, bf16[512,384]{1,0:T(8,128)(2,1)}) custom-call(s32[1]{0:T(128)} %bitcast.8.set_ref, bf16[4,2,64,1024]{3,2,1,0:T(8,128)(2,1)S(1)} %collective-permute-done.7.err_ref, bf16[384,256]{1,0:T(8,128)(2,1)S(1)} %maximum_bitcast_fusion.lat_ref, bf16[2,384,1024]{2,1,0:T(8,128)(2,1)S(1)} %bitcast.16, ...), custom_call_target="tpu_custom_call" | custom-call | flops 805306368 | bytes 2000000 | tf_op jit(solution)/shard_map/pallas_call | solution.py:187
  (7 shorter events, 0.1 us)
Async XLA Ops:
  0.6 3.6 %copy-start.2 = (bf16[1,16,1024]{2,1,0:T(8,128)(2,1)S(1)}, bf16[1,16,1024]{2,1,0:T(8,128)(2,1)}, u32[]{:S(2)}) copy-start(bf16[1,16,1024]{2,1,0:T(8,128)(2,1)} %param.5) | copy-start | bytes 98308
  2.3 26.7 %collective-permute-start = (bf16[1296,1024]{1,0:T(8,128)(2,1)S(1)}, bf16[1296,1024]{1,0:T(8,128)(2,1)S(1)}, u32[]{:S(2)}, u32[]{:S(2)}) collective-permute-start(bf16[1296,1024]{1,0:T(8,128)(2,1)S(1)} %shard_map.76.own_ref), channel_id=1, source_target_pairs={{0,1},{1,0},{2,3},{3,2},{4,5},{5,4},{6,7},{7,6},{8,9},{9,8},{10,11... | collective-permute-start | bytes 7962632 | tf_op jit(solution)/shard_map/ppermute | solution.py:21
  43.8 26.3 %copy-start.1 = (bf16[1,16,1024]{2,1,0:T(8,128)(2,1)S(1)}, bf16[1,16,1024]{2,1,0:T(8,128)(2,1)}, u32[]{:S(2)}) copy-start(bf16[1,16,1024]{2,1,0:T(8,128)(2,1)} %param.6) | copy-start | bytes 98308
  63.2 6.9 %collective-permute-start.1 = (bf16[64,1024]{1,0:T(8,128)(2,1)S(1)}, bf16[64,1024]{1,0:T(8,128)(2,1)S(1)}, u32[]{:S(2)}, u32[]{:S(2)}) collective-permute-start(bf16[64,1024]{1,0:T(8,128)(2,1)S(1)} %slice.23), channel_id=1, source_target_pairs={{0,32},{32,64},{64,96},{96,128},{128,160},{160,192},{192,224},{224... | collective-permute-start | bytes 393224 | tf_op jit(solution)/shard_map/ppermute | solution.py:37
  70.2 14.1 %collective-permute-start.2 = (bf16[64,1024]{1,0:T(8,128)(2,1)S(1)}, bf16[64,1024]{1,0:T(8,128)(2,1)S(1)}, u32[]{:S(2)}, u32[]{:S(2)}) collective-permute-start(bf16[64,1024]{1,0:T(8,128)(2,1)S(1)} %convert_element_type.35), channel_id=1, source_target_pairs={{0,9},{1,24},{3,10},{2,27},{4,13},{5,28},{7,14},{6,31},{9,0},{8,17... | collective-permute-start | bytes 393224 | tf_op jit(solution)/shard_map/ppermute | solution.py:31
  72.5 6.2 %collective-permute-start.3 = (bf16[128,384]{0,1:T(8,128)(2,1)S(1)}, bf16[128,384]{0,1:T(8,128)(2,1)S(1)}, u32[]{:S(2)}, u32[]{:S(2)}) collective-permute-start(bf16[128,384]{0,1:T(8,128)(2,1)S(1)} %get-tuple-element.42), channel_id=1, source_target_pairs={{0,1},{1,0},{2,3},{3,2},{4,5},{5,4},{6,7},{7,6},{8,9},{9,8},{10,11... | collective-permute-start | bytes 294920 | tf_op jit(solution)/shard_map/ppermute | solution.py:21
  76.7 46.2 %copy-start = (bf16[1,2,384,1024]{3,2,1,0:T(8,128)(2,1)S(1)}, bf16[1,2,384,1024]{3,2,1,0:T(8,128)(2,1)}, u32[]{:S(2)}) copy-start(bf16[1,2,384,1024]{3,2,1,0:T(8,128)(2,1)} %param.9) | copy-start | bytes 4718596
  76.7 3.3 %collective-permute-start.4 = (bf16[128,384]{0,1:T(8,128)(2,1)S(1)}, bf16[128,384]{0,1:T(8,128)(2,1)S(1)}, u32[]{:S(2)}, u32[]{:S(2)}) collective-permute-start(bf16[128,384]{0,1:T(8,128)(2,1)S(1)} %get-tuple-element.41), channel_id=1, source_target_pairs={{0,1},{1,0},{2,3},{3,2},{4,5},{5,4},{6,7},{7,6},{8,9},{9,8},{10,11... | collective-permute-start | bytes 294920 | tf_op jit(solution)/shard_map/ppermute | solution.py:21
  84.4 11.5 %collective-permute-start.5 = (bf16[64,1024]{1,0:T(8,128)(2,1)S(1)}, bf16[64,1024]{1,0:T(8,128)(2,1)S(1)}, u32[]{:S(2)}, u32[]{:S(2)}) collective-permute-start(bf16[64,1024]{1,0:T(8,128)(2,1)S(1)} %fusion), channel_id=1, source_target_pairs={{0,25},{1,8},{3,26},{2,11},{4,29},{5,12},{7,30},{6,15},{9,16},{8,1... | collective-permute-start | bytes 393224 | tf_op jit(solution)/shard_map/ppermute | solution.py:31
  95.9 9.0 %collective-permute-start.6 = (bf16[64,1024]{1,0:T(8,128)(2,1)S(1)}, bf16[64,1024]{1,0:T(8,128)(2,1)S(1)}, u32[]{:S(2)}, u32[]{:S(2)}) collective-permute-start(bf16[64,1024]{1,0:T(8,128)(2,1)S(1)} %get-tuple-element.39.own_ref), channel_id=1, source_target_pairs={{32,0},{64,32},{96,64},{128,96},{160,128},{192,160},{224,192},{256... | collective-permute-start | bytes 393224 | tf_op jit(solution)/shard_map/ppermute | solution.py:37
  120.9 4.8 %collective-permute-start.7 = (bf16[4,2,64,1024]{3,2,1,0:T(8,128)(2,1)}, bf16[4,2,64,1024]{3,2,1,0:T(8,128)(2,1)S(1)}, u32[]{:S(2)}, u32[]{:S(2)}) collective-permute-start(bf16[4,2,64,1024]{3,2,1,0:T(8,128)(2,1)} %all_to_all.11.err_ref), channel_id=1, source_target_pairs={{0,1},{1,0},{2,3},{3,2},{4,5},{5,4},{6,7},{7,6},{8,9},{9,8},{10,11... | collective-permute-start | bytes 3145736 | tf_op jit(solution)/shard_map/ppermute | solution.py:21
